TPU v7x, 256 devices: a whole 4x4x8 slice. The times are simulated.
256 devices in a mesh: gy: 16 (over y, x_hi, core), gz: 16 (over z, x_lo).
Axes of the slice: x: 4 (x_hi: 2, x_lo: 2; x = x_hi * 2 + x_lo), y: 4, z: 8, core: 2. Of those that a mesh axis runs over, the one named last changes fastest.
Arguments:
- labels: int32 [6, 4096, 2048], P(None, 'gy', 'gz'), may hold values from 0 to 5
- porosity: float32 [6], replicated, may hold values from 0 to 1
Outputs:
- spectra: float32 [4, 2, 4096, 2048], P(None, None, 'gy', 'gz')
All inputs are finite; a program needn't handle non-finite values.
Results may differ from a plain program's by a relative error of at most 0.0003.
Values sent between devices are 32-bit elements; how exact they have to be, the bound alone decides.
No kernel may reach another device: no remote copies, remote signals or barrier semaphores. Data moves between devices by JAX's collectives and lax.ppermute only.
A program may use at most 128 MiB of HBM per device.

v0:
```python
import math

import jax
import jax.numpy as jnp
from jax import lax
from jax.sharding import PartitionSpec as P


def extended(cells, sides, width):
    for axis, dim in sides:
        count = lax.axis_size(axis)
        head = lax.slice_in_dim(cells, 0, width, axis=dim)
        tail = lax.slice_in_dim(cells, cells.shape[dim] - width, cells.shape[dim], axis=dim)
        cells = jnp.concatenate(
            [
                lax.ppermute(tail, axis, [(i, (i + 1) % count) for i in range(count)]),
                cells,
                lax.ppermute(head, axis, [((i + 1) % count, i) for i in range(count)]),
            ],
            axis=dim,
        )
    return cells


def smooth_along(field, axis):
    extent = field.shape[axis]
    lower = lax.slice_in_dim(field, 0, extent - 2, axis=axis)
    middle = lax.slice_in_dim(field, 1, extent - 1, axis=axis)
    upper = lax.slice_in_dim(field, 2, extent, axis=axis)
    return (lower + 6.0 * middle + upper) * 0.125


def surface_pore(padded):
    smoothed = smooth_along(smooth_along(smooth_along(padded, 0), 1), 2)
    inner = smoothed[1:-1, 1:-1, 1:-1]
    grad_x = smoothed[2:, 1:-1, 1:-1] - smoothed[:-2, 1:-1, 1:-1]
    grad_y = smoothed[1:-1, 2:, 1:-1] - smoothed[1:-1, :-2, 1:-1]
    grad_z = smoothed[1:-1, 1:-1, 2:] - smoothed[1:-1, 1:-1, :-2]
    surface = jnp.sqrt(grad_x * grad_x + grad_y * grad_y + grad_z * grad_z + 0.01)
    return (surface, inner)


def angles(wave_numbers, positions, length):
    product = wave_numbers[:, None] * positions[None, :] % length
    return product.astype(jnp.float32) * (2.0 * math.pi / length)


def shards(labels, porosity):
    phase_count = porosity.shape[0]
    phase_ids = jnp.arange(phase_count, dtype=jnp.int32)
    filled = jnp.sum(jnp.where(labels[..., None] == phase_ids, porosity, 0.0), axis=-1)
    padded = extended(filled, (("gy", 1), ("gz", 2)), 2)
    surface, pore_field = surface_pore(padded)
    fields = jnp.stack([surface, pore_field])
    cells_y = fields.shape[2]
    cells_z = fields.shape[3]
    total_y = cells_y * lax.axis_size("gy")
    total_z = cells_z * lax.axis_size("gz")
    index_y = lax.axis_index("gy")
    index_z = lax.axis_index("gz")
    highest = lax.Precision.HIGHEST
    zeros_y = jnp.zeros(fields.shape, jnp.float32)
    modes_y = index_y * cells_y + jnp.arange(cells_y, dtype=jnp.int32)
    block_rows = lax.all_gather(fields, "gy", axis=2, tiled=True)
    positions = jnp.arange(block_rows.shape[2], dtype=jnp.int32)
    theta = angles(modes_y, positions, total_y)
    cosine = jnp.einsum("my,fxyz->fxmz", jnp.cos(theta), block_rows, precision=highest)
    sine = jnp.einsum("my,fxyz->fxmz", jnp.sin(theta), block_rows, precision=highest)
    trans_re = cosine
    trans_im = (zeros_y, zeros_y)[1] - sine
    modes_z = index_z * cells_z + jnp.arange(cells_z, dtype=jnp.int32)
    block_re = lax.all_gather(trans_re, "gz", axis=3, tiled=True)
    block_im = lax.all_gather(trans_im, "gz", axis=3, tiled=True)
    positions = jnp.arange(block_re.shape[3], dtype=jnp.int32)
    theta = angles(modes_z, positions, total_z)
    cosine = jnp.cos(theta)
    sine = jnp.sin(theta)
    next_re = jnp.einsum("fxmz,kz->fxmk", block_re, cosine, precision=highest) + jnp.einsum(
        "fxmz,kz->fxmk", block_im, sine, precision=highest
    )
    next_im = jnp.einsum("fxmz,kz->fxmk", block_im, cosine, precision=highest) - jnp.einsum(
        "fxmz,kz->fxmk", block_re, sine, precision=highest
    )
    surf_re, pore_re = (next_re[0], next_re[1])
    surf_im, pore_im = (next_im[0], next_im[1])
    factor = 64.0 / (total_y * total_z)
    spectra = jnp.stack(
        [
            (surf_re * surf_re + surf_im * surf_im) * factor,
            (pore_re * pore_re + pore_im * pore_im) * factor,
            (surf_re * pore_re + surf_im * pore_im) * factor,
            (surf_im * pore_re - surf_re * pore_im) * factor,
        ]
    )
    local_y = lax.broadcasted_iota(jnp.int32, (cells_y, cells_z), 0) + index_y * cells_y
    local_z = lax.broadcasted_iota(jnp.int32, (cells_y, cells_z), 1) + index_z * cells_z
    anchor = jnp.logical_and(local_y == 0, local_z == 0)
    return jnp.where(anchor, 0.0, spectra)


def solution(mesh):
    placed = (P(None, "gy", "gz"), P())
    return jax.shard_map(
        shards, mesh=mesh, in_specs=placed, out_specs=P(None, None, "gy", "gz"), check_vma=False
    )
```

profile of v0, /device:TPU:1, one launch (start us, length us, event | category | flops | bytes accessed | tf_op | source)
XLA Modules:
  0.0 571.6 jit_solution(2140689222321485766)
XLA Ops:
  6.5 0.0 all-gather.4.cloned.1.call-start
  6.5 1.8 select_reduce_fusion
  8.3 0.2 copy.7
  8.5 4.2 collective-permute-start
  12.7 0.2 copy.8
  12.9 0.1 collective-permute-start.1
  13.0 0.3 copy.9
  13.3 4.2 collective-permute-done
  17.4 6.2 %collective-permute-done.1 = f32[6,2,128]{1,2,0:T(8,128)S(1)} collective-permute-done((f32[6,2,128]{1,2,0:T(8,128)S(1)}, f32[6,2,128]{1,2,0:T(8,128)S(1)}, u32[]{:S(2)}, u32[]{:S(2)}) %collective-permute-start.1) | collective-permute-done | bytes 6176 | tf_op jit(solution)/shard_map/ppermute | solution.py:18
  23.6 0.1 pad_maximum_fusion.4
  23.8 1.0 collective-permute-start.2
  24.7 5.4 collective-permute-start.3
  30.1 1.1 collective-permute-done.2
  31.2 0.0 collective-permute-done.3
  31.2 0.5 pad_maximum_fusion
  31.7 0.1 fusion.39
  31.8 0.5 fusion.37
  32.3 0.2 fusion.35
  32.6 0.5 fusion.51
  33.1 0.8 pad_maximum_fusion.1
  33.9 0.0 all-gather.4.cloned.1.call-update
  33.9 0.2 all-gather.6.cloned.1.call-start
  34.2 82.0 %all-gather.4.cloned.1.call-done = f32[2,2,4096,128]{2,3,1,0:T(8,128)} async-done(((f32[2,2,256,128]{2,3,1,0:T(8,128)}), f32[2,2,4096,128]{2,3,1,0:T(8,128)}) %all-gather.4.cloned.1.call-update) | async-done | bytes 8388624 | tf_op jit(solution)/shard_map/all_gather | solution.py:64
  116.1 25.1 %fusion.14 = f32[2,2,256,128]{2,3,1,0:T(8,128)} fusion(f32[2,2,4096,128]{2,3,1,0:T(8,128)} %all-gather.4.cloned.1.call-done, s32[256]{0:T(256)S(1)} %iota_add_fusion), kind=kOutput, calls=%fused_computation.21 | convolution fusion | flops 6457131008 | bytes 8913920 | tf_op jit(solution)/shard_map/my,fxyz->fxmz/dot_general | solution.py:67
  141.2 0.0 all-gather.6.cloned.1.call-update
  141.2 0.0 all-gather.8.cloned.1.call-start
  141.3 25.4 %fusion.20 = f32[2,2,256,128]{2,3,1,0:T(8,128)} fusion(f32[2,2,4096,128]{2,3,1,0:T(8,128)} %all-gather.4.cloned.1.call-done, s32[256]{0:T(256)S(1)} %iota_add_fusion), kind=kOutput, calls=%fused_computation.25 | convolution fusion | flops 6457262080 | bytes 8913920 | tf_op jit(solution)/shard_map/my,fxyz->fxmz/dot_general | solution.py:68
  166.7 0.0 all-gather.8.cloned.1.call-update
  166.8 0.1 broadcast_and_fusion
  166.9 154.2 %all-gather.6.cloned.1.call-done = f32[2,2,256,2048]{2,3,1,0:T(8,128)} async-done(((f32[2,2,256,128]{2,3,1,0:T(8,128)}), f32[2,2,256,2048]{2,3,1,0:T(8,128)}) %all-gather.6.cloned.1.call-update) | async-done | bytes 8388624 | tf_op jit(solution)/shard_map/all_gather | solution.py:72
  321.0 20.1 %fusion.30 = f32[2,2,256,128]{3,2,1,0:T(8,128)S(1)} fusion(f32[2,2,256,2048]{2,3,1,0:T(8,128)} %all-gather.6.cloned.1.call-done, s32[128]{0:T(128)S(1)} %iota_add_fusion.1), kind=kOutput, calls=%fused_computation.34 | convolution fusion | flops 3224895488 | bytes 8913408 | tf_op jit(solution)/shard_map/fxmz,kz->fxmk/dot_general | solution.py:78
  341.1 165.4 %all-gather.8.cloned.1.call-done = f32[2,2,256,2048]{2,3,1,0:T(8,128)} async-done(((f32[2,2,256,128]{2,3,1,0:T(8,128)}), f32[2,2,256,2048]{2,3,1,0:T(8,128)}) %all-gather.8.cloned.1.call-update) | async-done | bytes 8388624 | tf_op jit(solution)/shard_map/all_gather | solution.py:73
  506.5 0.0 slice-start
  506.5 20.0 %fusion.28 = f32[2,2,256,128]{3,2,1,0:T(8,128)S(1)} fusion(f32[2,2,256,2048]{2,3,1,0:T(8,128)} %all-gather.8.cloned.1.call-done, s32[128]{0:T(128)S(1)} %iota_add_fusion.1), kind=kOutput, calls=%fused_computation.32 | convolution fusion | flops 3224895488 | bytes 8913408 | tf_op jit(solution)/shard_map/fxmz,kz->fxmk/dot_general | solution.py:81
  526.5 0.0 slice-start.1
  526.6 20.2 %convolution_add_fusion = f32[2,2,256,128]{3,2,1,0:T(8,128)S(1)} fusion(f32[2,2,256,128]{3,2,1,0:T(8,128)S(1)} %fusion.30, f32[2,2,256,2048]{2,3,1,0:T(8,128)} %all-gather.8.cloned.1.call-done, s32[128]{0:T(128)S(1)} %iota_add_fusion.1), kind=kOutput, calls=%fused_computation.23 | convolution fusion | flops 3225026560 | bytes 9437696 | tf_op jit(solution)/shard_map/fxmz,kz->fxmk/dot_general | solution.py:78
  546.7 0.0 slice-done
  546.7 0.0 slice-done.1
  546.8 17.0 %convolution_subtract_fusion = f32[2,2,256,128]{3,2,1,0:T(8,128)S(1)} fusion(f32[2,2,256,128]{3,2,1,0:T(8,128)S(1)} %fusion.28, f32[2,2,256,2048]{2,3,1,0:T(8,128)S(1)} %bitcast.45, s32[128]{0:T(128)S(1)} %iota_add_fusion.1), kind=kOutput, calls=%fused_computation.22 | convolution fusion | flops 3225026560 | bytes 9437696 | tf_op jit(solution)/shard_map/fxmz,kz->fxmk/dot_general | solution.py:81
  563.7 0.1 add_multiply_fusion.2
  563.9 1.1 maximum_select_fusion
  (6 shorter events, 0.0 us)
Async XLA Ops:
  6.5 109.6 %all-gather.4.cloned.1.call-start = ((), (), s32[]{:S(2)}) async-start(), calls=%async_computation | async-start | bytes 8912896 | tf_op jit(solution)/shard_map/all_gather | solution.py:64
  8.5 8.9 %collective-permute-start = (f32[6,2,128]{1,2,0:T(8,128)S(1)}, f32[6,2,128]{1,2,0:T(8,128)S(1)}, u32[]{:S(2)}, u32[]{:S(2)}) collective-permute-start(f32[6,2,128]{1,2,0:T(8,128)S(1)} %copy.7), channel_id=1, source_target_pairs={{0,16},{16,32},{32,48},{48,64},{64,80},{80,96},{96,112},{112,128},... | collective-permute-start | bytes 18440 | tf_op jit(solution)/shard_map/ppermute | solution.py:16
  12.9 10.7 %collective-permute-start.1 = (f32[6,2,128]{1,2,0:T(8,128)S(1)}, f32[6,2,128]{1,2,0:T(8,128)S(1)}, u32[]{:S(2)}, u32[]{:S(2)}) collective-permute-start(f32[6,2,128]{1,2,0:T(8,128)S(1)} %copy.8), channel_id=1, source_target_pairs={{16,0},{32,16},{48,32},{64,48},{80,64},{96,80},{112,96},{128,112},... | collective-permute-start | bytes 18440 | tf_op jit(solution)/shard_map/ppermute | solution.py:18
  23.8 7.4 %collective-permute-start.2 = (f32[6,260,2]{1,2,0:T(2,128)S(1)}, f32[6,260,2]{1,2,0:T(2,128)S(1)}, u32[]{:S(2)}, u32[]{:S(2)}) collective-permute-start(f32[6,260,2]{1,2,0:T(2,128)S(1)} %get-tuple-element.5), channel_id=1, source_target_pairs={{0,1},{1,2},{2,3},{3,4},{4,5},{5,6},{6,7},{7,8},{8,9},{9,10},{10,1... | collective-permute-start | bytes 37448 | tf_op jit(solution)/shard_map/ppermute | solution.py:16
  24.7 6.4 %collective-permute-start.3 = (f32[6,260,2]{1,2,0:T(2,128)S(1)}, f32[6,260,2]{1,2,0:T(2,128)S(1)}, u32[]{:S(2)}, u32[]{:S(2)}) collective-permute-start(f32[6,260,2]{1,2,0:T(2,128)S(1)} %get-tuple-element.6), channel_id=1, source_target_pairs={{1,0},{2,1},{3,2},{4,3},{5,4},{6,5},{7,6},{8,7},{9,8},{10,9},{11,1... | collective-permute-start | bytes 37448 | tf_op jit(solution)/shard_map/ppermute | solution.py:18
  33.9 287.1 %all-gather.6.cloned.1.call-start = ((), (), s32[]{:S(2)}) async-start(), calls=%async_computation.1 | async-start | bytes 8912896 | tf_op jit(solution)/shard_map/all_gather | solution.py:72
  141.2 365.3 %all-gather.8.cloned.1.call-start = ((), (), s32[]{:S(2)}) async-start(), calls=%async_computation.2 | async-start | bytes 8912896 | tf_op jit(solution)/shard_map/all_gather | solution.py:73
  506.5 40.2 %slice-start = ((s8[8388608]{0:T(1024)(128)(4,1)}), s8[4194304]{0:T(1024)(128)(4,1)S(1)}, s32[]{:S(2)}) async-start(s8[8388608]{0:T(1024)(128)(4,1)} %bitcast.44), calls=%async_computation.3 | async-start | bytes 8388608
  526.5 20.2 %slice-start.1 = ((s8[8388608]{0:T(1024)(128)(4,1)}), s8[4194304]{0:T(1024)(128)(4,1)S(1)}, s32[]{:S(2)}) async-start(s8[8388608]{0:T(1024)(128)(4,1)} %bitcast.44), calls=%async_computation.4 | async-start | bytes 8388608
Sparse Core Ops, SparseCore 0:
  34.1 82.0 all-gather.3
  141.4 179.6 all-gather.5
  322.8 183.6 all-gather.7
where the time goes:
time: 577 us; the launch traced here: 572 us
  waiting for transfers between devices  413 us (72%)
  matrix products  128 us (22%)
  between operations  13.5 us (2%)
  starting transfers between devices  10.9 us (2%)
  other arithmetic  5.88 us (1%)
    all_gather x1, waiting for transfers between devices, shards(): block_im = lax.all_gather(trans_im, 'gz', axis=3, tiled=True)  165 us
    all_gather x1, waiting for transfers between devices, shards(): block_re = lax.all_gather(trans_re, 'gz', axis=3, tiled=True)  154 us
    all_gather x1, waiting for transfers between devices, shards(): block_rows = lax.all_gather(fields, 'gy', axis=2, tiled=True)  82 us
    dot_general x1, matrix products, shards(): jnp.einsum('my,fxyz->fxmz', jnp.sin(theta), block_rows, precision=highest)  25.4 us
    dot_general x1, matrix products, shards(): jnp.einsum('my,fxyz->fxmz', jnp.cos(theta), block_rows, precision=highest)  25.1 us
    dot_general x1, matrix products, shards(): jnp.einsum('fxmz,kz->fxmk', block_im, sine, precision=highest)  20.2 us
    dot_general x1, matrix products, shards(): jnp.einsum('fxmz,kz->fxmk', block_re, cosine, precision=highest)  20.1 us
    dot_general x1, matrix products, shards(): jnp.einsum('fxmz,kz->fxmk', block_im, cosine, precision=highest)  20 us
  transfers between devices with their start and end apart: 7, of which 6 were waited for; matrix products, arithmetic and copies ran while one was open for 8% of the time, Pallas kernels for 0%

commit v1 on v0

v1 whole, which is shorter than its diff:
```python
import functools
import math

import jax
import jax.numpy as jnp
import ml_dtypes
import numpy as np
from jax import lax
from jax.experimental import pallas as pl
from jax.experimental.pallas import tpu as pltpu
from jax.sharding import PartitionSpec as P

VMEM = pl.BlockSpec(memory_space=pltpu.VMEM)
SMEM = pl.BlockSpec(memory_space=pltpu.SMEM)
PARAMS = pltpu.CompilerParams(vmem_limit_bytes=48 * 1024 * 1024)


def halves(matrix):
    high = matrix.astype(ml_dtypes.bfloat16)
    low = (matrix - high.astype(np.float64)).astype(ml_dtypes.bfloat16)
    return high, low


def split(value):
    high = value.astype(jnp.bfloat16)
    low = (value - high.astype(jnp.float32)).astype(jnp.bfloat16)
    return high, low


def dot(a, b):
    return lax.dot_general(a, b, (((1,), (0,)), ((), ())), preferred_element_type=jnp.float32)


def dot_t(a, b):
    return lax.dot_general(a, b, (((1,), (1,)), ((), ())), preferred_element_type=jnp.float32)


def z_matrices():
    q = np.arange(128)[:, None]
    j = np.arange(128)[None, :]

    def block(s, sign):
        theta = 2.0 * math.pi / 2048 * ((j * (16 * q + s)) % 2048)
        return np.concatenate([np.cos(theta), sign * np.sin(theta)], axis=1)

    entries = []
    for e in range(8):
        first = block(e, 1.0)
        second = block(8, 1.0) if e == 0 else block(16 - e, -1.0)
        high_a, low_a = halves(first)
        high_b, low_b = halves(second)
        entries.append(np.concatenate([high_a, high_b, low_a, low_b], axis=0))
    return np.stack(entries)


def y_matrix():
    m = np.arange(256)[:, None]
    i = np.arange(256)[None, :]
    theta = 2.0 * math.pi / 256 * ((m * i) % 256)
    high, low = halves(np.concatenate([np.cos(theta), np.sin(theta)], axis=0))
    return np.concatenate([high, low], axis=0)


def twiddles():
    m = np.arange(256)[:, None]
    r = np.arange(128)[None, :] % 16
    phi = 2.0 * math.pi / 4096 * (m * r)
    return np.cos(phi).astype(np.float32), (-np.sin(phi)).astype(np.float32)


def last_matrix():
    w = np.zeros((4, 2, 16, 2, 2, 2, 2, 16))
    g = np.arange(16)[:, None]
    r = np.arange(16)[None, :]
    psi = 2.0 * math.pi / 16 * ((g * r) % 16)
    cos, sin = np.cos(psi), np.sin(psi)
    for field in range(2):
        for plane in range(2):
            w[2 * field, plane, :, 0, 0, field, plane] = cos
            w[2 * field, plane, :, 1, 1, field, plane] = cos
            w[2 * field, plane, :, 0, 1, field, plane] = sin
            w[2 * field, plane, :, 1, 0, field, plane] = -sin
            w[2 * field + 1, plane, :, 0, 1, field, plane] = cos
            w[2 * field + 1, plane, :, 1, 0, field, plane] = -cos
            w[2 * field + 1, plane, :, 0, 0, field, plane] = -sin
            w[2 * field + 1, plane, :, 1, 1, field, plane] = -sin
    high, low = halves(w.reshape(128, 256))
    return np.concatenate([high, low], axis=0)


def rows_kernel(por_ref, lab_ref, up_ref, down_ref, out_ref, ext):
    def fill(ids):
        value = jnp.full(ids.shape, por_ref[0], jnp.float32)
        for k in range(1, 6):
            value = jnp.where(ids == k, por_ref[k], value)
        return value

    def along_x(ref):
        f = [fill(ref[x]) for x in range(6)]
        s = [(f[k] + 6.0 * f[k + 1] + f[k + 2]) * 0.125 for k in range(4)]
        return [s[2] - s[0], s[3] - s[1], s[1], s[2]]

    for a, value in enumerate(along_x(lab_ref)):
        ext[a, 8:264, :] = value
    for a, value in enumerate(along_x(up_ref)):
        ext[a, 6:8, :] = value
    for a, value in enumerate(along_x(down_ref)):
        ext[a, 264:266, :] = value
    for a in range(4):
        main = (ext[a, 7:263, :] + 6.0 * ext[a, 8:264, :] + ext[a, 9:265, :]) * 0.125
        out_ref[:, 16 * a : 16 * a + 16, :] = main.reshape(16, 16, 128)
    for p in range(2):
        a = 2 + p
        first = (ext[a, 6:7, :] + 6.0 * ext[a, 7:8, :] + ext[a, 8:9, :]) * 0.125
        last = (ext[a, 263:264, :] + 6.0 * ext[a, 264:265, :] + ext[a, 265:266, :]) * 0.125
        for d in range(16):
            below = first if d == 0 else out_ref[d - 1, 16 * a + 15 : 16 * a + 16, :]
            above = last if d == 15 else out_ref[d + 1, 16 * a : 16 * a + 1, :]
            out_ref[d, 64 + 2 * p : 65 + 2 * p, :] = below
            out_ref[d, 65 + 2 * p : 66 + 2 * p, :] = above
    out_ref[:, 68:72, :] = jnp.zeros((16, 4, 128), jnp.float32)


def real_transform(x):
    n = len(x)
    if n == 2:
        return [(x[0] + x[1], None), (x[0] - x[1], None)]
    even = real_transform(x[0::2])
    odd = real_transform(x[1::2])
    out = [None] * (n // 2 + 1)
    for k in range(n // 4 + 1):
        (er, ei), (dr, di) = even[k], odd[k]
        c, s = math.cos(2.0 * math.pi * k / n), math.sin(2.0 * math.pi * k / n)
        if k == 0:
            out[0] = (er + dr, None)
            out[n // 2] = (er - dr, None)
        elif 4 * k == n:
            out[k] = (er, -dr)
        else:
            tr = c * dr if di is None else c * dr + s * di
            ti = -s * dr if di is None else c * di - s * dr
            out[k] = (er + tr, ti if ei is None else ei + ti)
            out[n // 2 - k] = (er - tr, ti if ei is None else ti - ei)
    return out


def columns_kernel(in_ref, w_ref, out_ref, ext, x_ref):
    lane = lax.broadcasted_iota(jnp.int32, (16, 16, 128), 2)

    def before(x):
        rolled = pltpu.roll(x, 1, 2)
        return jnp.where(lane == 0, jnp.concatenate([rolled[15:], rolled[:15]], axis=0), rolled)

    def after(x):
        rolled = pltpu.roll(x, 127, 2)
        return jnp.where(lane == 127, jnp.concatenate([rolled[1:], rolled[:1]], axis=0), rolled)

    def along_z(x):
        return (before(x) + 6.0 * x + after(x)) * 0.125

    for p in range(2):
        center = in_ref[:, 32 + 16 * p : 48 + 16 * p, :]
        ext[:, 8:24, :] = center
        ext[:, 7:8, :] = in_ref[:, 64 + 2 * p : 65 + 2 * p, :]
        ext[:, 24:25, :] = in_ref[:, 65 + 2 * p : 66 + 2 * p, :]
        grad_x = along_z(in_ref[:, 16 * p : 16 * p + 16, :])
        grad_y = along_z(ext[:, 9:25, :] - ext[:, 7:23, :])
        pore = along_z(center)
        grad_z = after(pore) - before(pore)
        surface = jnp.sqrt(grad_x * grad_x + grad_y * grad_y + grad_z * grad_z + 0.01)
        x_ref[:, 16 * p : 16 * p + 16, :] = surface
        x_ref[:, 32 + 16 * p : 48 + 16 * p, :] = pore
    parts = real_transform([x_ref[d] for d in range(16)])
    sign = jnp.where(lax.broadcasted_iota(jnp.int32, (128, 128), 1) < 64, 1.0, -1.0)

    def arranged(k):
        re, im = parts[k]
        if im is None:
            im = jnp.zeros_like(re)
        top = jnp.concatenate([re, im], axis=1)
        bottom = jnp.concatenate([im, -re], axis=1)
        return split(jnp.concatenate([top, bottom], axis=0))

    for k in (0, 8):
        high, low = arranged(k)
        at = 16 * k
        lead = w_ref[0, at : at + 128, :]
        tail = w_ref[0, at + 256 : at + 384, :]
        out_ref[k] = dot_t(lead, high) + dot_t(tail, high) + dot_t(lead, low)
    for k in range(1, 8):
        high, low = arranged(k)
        main = dot_t(w_ref[k], high)
        both = main[:256] + main[256:] + dot_t(w_ref[k, :256, :], low)
        out_ref[k] = both[:128]
        out_ref[16 - k] = both[128:] * sign


def spectra_kernel(in_ref, y_ref, tr_ref, ti_ref, last_ref, out_ref):
    factor = 64.0 / (4096 * 2048)
    for q in range(8):
        high, low = split(in_ref[pl.ds(q, 256, stride=8), :])
        main = dot(y_ref[...], high)
        both = main[:512] + main[512:] + dot(y_ref[:512, :], low)
        cos, sin = both[:256], both[256:]
        tr, ti = tr_ref[...], ti_ref[...]
        mixed = jnp.concatenate([cos * tr + sin * ti, sin * tr - cos * ti], axis=1)
        high, low = split(mixed)
        main = dot_t(last_ref[...], high)
        modes = main[:128] + main[128:] + dot_t(last_ref[:128, :], low)
        sr, si, pr, pi = modes[:32], modes[32:64], modes[64:96], modes[96:]
        results = (
            (sr * sr + si * si) * factor,
            (pr * pr + pi * pi) * factor,
            (sr * pr + si * pi) * factor,
            (si * pr - sr * pi) * factor,
        )
        for o, result in enumerate(results):
            for p in range(2):
                for half in range(2):
                    start = 8 * (2 * q + half) + 2 * o + p
                    block = result[16 * p : 16 * p + 16, 128 * half : 128 * half + 128]
                    out_ref[pl.ds(start, 16, stride=128), :] = block


def order_kernel(first_ref, in_ref, out_ref):
    row = lax.broadcasted_iota(jnp.int32, (128, 128), 0)
    col = lax.broadcasted_iota(jnp.int32, (128, 128), 1)
    drop = jnp.logical_and(row + col == 0, first_ref[0] == 1)
    for o in range(8):
        for half in range(2):
            parts = [in_ref[pl.ds(8 * (2 * q + half) + o, 16, stride=128), :] for q in range(8)]
            block = jnp.concatenate(parts, axis=0).T
            if half == 0:
                block = jnp.where(drop, 0.0, block)
            out_ref[o, 128 * half : 128 * half + 128, :] = block


def shape(*sizes):
    return jax.ShapeDtypeStruct(sizes, jnp.float32)


def shards(labels, porosity):
    count = lax.axis_size("gy")
    up = lax.ppermute(labels[:, -2:, :], "gy", [(i, (i + 1) % count) for i in range(count)])
    down = lax.ppermute(labels[:, :2, :], "gy", [((i + 1) % count, i) for i in range(count)])
    rows = pl.pallas_call(
        rows_kernel,
        out_shape=shape(16, 72, 128),
        in_specs=[SMEM, VMEM, VMEM, VMEM],
        out_specs=VMEM,
        scratch_shapes=[pltpu.VMEM((4, 272, 128), jnp.float32)],
        compiler_params=PARAMS,
        name="rows",
    )(porosity, labels, up, down)
    rows = lax.all_to_all(rows, "gz", 0, 0, tiled=True)
    columns = pl.pallas_call(
        columns_kernel,
        out_shape=shape(16, 128, 128),
        in_specs=[VMEM, VMEM],
        out_specs=VMEM,
        scratch_shapes=[pltpu.VMEM((16, 32, 128), jnp.float32), pltpu.VMEM((16, 64, 128), jnp.float32)],
        compiler_params=PARAMS,
        name="columns",
    )(rows, jnp.asarray(z_matrices()))
    columns = lax.all_to_all(columns.reshape(256, 8, 128), ("gy", "gz"), 0, 0, tiled=True)
    cos, sin = twiddles()
    spectra = pl.pallas_call(
        spectra_kernel,
        out_shape=shape(2048, 128),
        in_specs=[VMEM] * 5,
        out_specs=VMEM,
        compiler_params=PARAMS,
        name="spectra",
    )(columns.reshape(2048, 128), jnp.asarray(y_matrix()), jnp.asarray(cos), jnp.asarray(sin), jnp.asarray(last_matrix()))
    spectra = lax.all_to_all(spectra.reshape(16, 128, 128), "gy", 0, 0, tiled=True)
    origin = jnp.logical_and(lax.axis_index("gy") == 0, lax.axis_index("gz") == 0).astype(jnp.int32).reshape(1)
    result = pl.pallas_call(
        order_kernel,
        out_shape=shape(8, 256, 128),
        in_specs=[SMEM, VMEM],
        out_specs=VMEM,
        compiler_params=PARAMS,
        name="order",
    )(origin, spectra.reshape(2048, 128))
    return result.reshape(4, 2, 256, 128)


def solution(mesh):
    placed = (P(None, "gy", "gz"), P())
    return jax.shard_map(
        shards, mesh=mesh, in_specs=placed, out_specs=P(None, None, "gy", "gz"), check_vma=False
    )
```

time: 577 us -> 111 us (0.19)
  waiting for transfers between devices: 413 us -> 22.1 us
  matrix products: 128 us -> 0 us
  blocking collectives: 0 us -> 65.6 us
  between operations: 13.5 us -> 0.05 us
  Pallas kernels: 0 us -> 11 us
  other arithmetic: 5.88 us -> 0 us
    all_gather x3 -> x0, waiting for transfers between devices: 402 us -> none  [the longest x1 165 us: shards(): block_im = lax.all_gather(trans_im, 'gz', axis=3, tiled=True)]
    dot_general x6 -> x0, matrix products: 128 us -> none  [the longest x1 25.4 us: shards(): jnp.einsum('my,fxyz->fxmz', jnp.sin(theta), block_rows, precision=highest)]
    all_to_all x0 -> x2, blocking collectives: none -> 65.6 us  [the longest x1 39 us: shards(): lax.all_to_all(columns.reshape(256, 8, 128), ('gy', 'gz'), 0, 0, tiled=True)]
    all_to_all x0 -> x1, waiting for transfers between devices: none -> 17.2 us  [shards(): lax.all_to_all(spectra.reshape(16, 128, 128), 'gy', 0, 0, tiled=True)]
    pallas_call x0 -> x4, Pallas kernels: none -> 11 us  [the longest x1 6.63 us: shards(): pl.pallas_call(spectra_kernel, out_shape=shape(2048, 128), in_specs=[VMEM...]
    ppermute x4 -> x2, waiting for transfers between devices: 11.4 us -> 4.85 us  [the longest x1 4.08 us: shards(): lax.ppermute(labels[:, :2, :], 'gy', [((i + 1) % count, i) for i in range...]
    ppermute x4 -> x2, starting transfers between devices: 10.7 us -> 4.14 us  [the longest x1 4.13 us: shards(): lax.ppermute(labels[:, -2:, :], 'gy', [(i, (i + 1) % count) for i in rang...]
  transfers between devices with their start and end apart: 7 -> 3, of which waited for: 6 -> 3; matrix products, arithmetic and copies ran while one was open for 8% -> 0% of each run, Pallas kernels for 0% -> 0%
where the time goes in v1:
time: 111 us; the launch traced here: 110 us
  blocking collectives  65.6 us (59%)
  waiting for transfers between devices  22.1 us (20%)
  Pallas kernels  11 us (10%)
  starting transfers between devices  8.84 us (8%)
  local copies, waits for them, and re-layouts  2.72 us (2%)
    all_to_all x1, blocking collectives, shards(): lax.all_to_all(columns.reshape(256, 8, 128), ('gy', 'gz'), 0, 0, tiled=True)  39 us
    all_to_all x1, blocking collectives, shards(): rows = lax.all_to_all(rows, 'gz', 0, 0, tiled=True)  26.6 us
    all_to_all x1, waiting for transfers between devices, shards(): lax.all_to_all(spectra.reshape(16, 128, 128), 'gy', 0, 0, tiled=True)  17.2 us
    pallas_call x1, Pallas kernels, shards(): pl.pallas_call(spectra_kernel, out_shape=shape(2048, 128), in_specs=[VMEM...  6.63 us
    all_to_all x1, starting transfers between devices, shards(): lax.all_to_all(spectra.reshape(16, 128, 128), 'gy', 0, 0, tiled=True)  4.7 us
    ppermute x1, starting transfers between devices, shards(): lax.ppermute(labels[:, -2:, :], 'gy', [(i, (i + 1) % count) for i in rang...  4.13 us
    ppermute x1, waiting for transfers between devices, shards(): lax.ppermute(labels[:, :2, :], 'gy', [((i + 1) % count, i) for i in range...  4.08 us
  transfers between devices with their start and end apart: 3, of which 3 were waited for; matrix products, arithmetic and copies ran while one was open for 0% of the time, Pallas kernels for 0%

profile of v1, /device:TPU:1, one launch (start us, length us, event | category | flops | bytes accessed | tf_op | source)
XLA Modules:
  0.0 110.3 jit_solution(15990139419221071252)
XLA Ops:
  0.0 0.0 copy-start
  0.0 0.9 fusion
  0.9 4.1 %collective-permute-start = (s32[6,2,128]{2,1,0:T(2,128)S(1)}, s32[6,2,128]{2,1,0:T(2,128)S(1)}, u32[]{:S(2)}, u32[]{:S(2)}) collective-permute-start(s32[6,2,128]{2,1,0:T(2,128)S(1)} %get-tuple-element.6), channel_id=1, source_target_pairs={{0,16},{16,32},{32,48},{48,64},{64,80},{80,96},{96,112},{112,128},... | collective-permute-start | bytes 18440 | tf_op jit(solution)/shard_map/ppermute | solution.py:244
  5.0 0.0 collective-permute-start.1
  5.0 0.8 collective-permute-done.up_ref
  5.8 4.1 %collective-permute-done.1.down_ref = s32[6,2,128]{2,1,0:T(2,128)S(1)} collective-permute-done((s32[6,2,128]{2,1,0:T(2,128)S(1)}, s32[6,2,128]{2,1,0:T(2,128)S(1)}, u32[]{:S(2)}, u32[]{:S(2)}) %collective-permute-start.1) | collective-permute-done | bytes 6176 | tf_op jit(solution)/shard_map/ppermute | solution.py:245
  9.9 0.0 copy-start.1
  9.9 1.1 %copy-done.1 = s32[6,256,128]{2,1,0:T(8,128)S(1)} copy-done((s32[6,256,128]{2,1,0:T(8,128)S(1)}, s32[6,256,128]{2,1,0:T(8,128)}, u32[]{:S(2)}) %copy-start.1) | copy-done | bytes 786456
  11.0 0.0 copy-start.6
  11.0 0.7 copy-done.6
  11.7 1.1 rows.1
  12.7 26.6 %all_to_all.15.in_ref = f32[16,72,128]{2,1,0:T(8,128)S(1)} all-to-all(f32[16,72,128]{2,1,0:T(8,128)S(1)} %rows.1), channel_id=1, replica_groups=mesh['gy'=16,'gz'=16] {'gz'}, dimensions={0} | all-to-all | bytes 1179648 | tf_op jit(solution)/shard_map/all_to_all | solution.py:255
  39.4 0.0 copy-done
  39.4 0.0 copy-start.2
  39.4 0.0 copy-start.3
  39.4 0.0 copy-start.4
  39.4 0.0 copy-start.5
  39.4 1.7 %columns.1 = f32[16,128,128]{2,1,0:T(8,128)S(1)} custom-call(f32[16,72,128]{2,1,0:T(8,128)S(1)} %all_to_all.15.in_ref, bf16[8,512,256]{2,1,0:T(8,128)(2,1)S(1)} %copy-done), custom_call_target="tpu_custom_call" | custom-call | tf_op jit(solution)/shard_map/columns/pallas_call | solution.py:256
  41.1 39.0 %all_to_all.16 = f32[256,8,128]{2,1,0:T(8,128)S(1)} all-to-all(f32[256,8,128]{2,1,0:T(8,128)S(1)} %bitcast.7), channel_id=1, replica_groups=mesh['gy'=16,'gz'=16] {'gy','gz'}, dimensions={0} | all-to-all | bytes 2097152 | tf_op jit(solution)/shard_map/all_to_all | solution.py:265
  80.1 0.0 copy-done.2
  80.2 0.0 copy-done.3
  80.2 0.0 copy-done.4
  80.2 0.0 copy-done.5
  80.2 6.6 %spectra.1 = f32[2048,128]{1,0:T(8,128)} custom-call(f32[2048,128]{1,0:T(8,128)S(1)} %bitcast.6, bf16[1024,256]{1,0:T(8,128)(2,1)S(1)} %copy-done.2, f32[256,128]{1,0:T(8,128)S(1)} %copy-done.3, f32[256,128]{1,0:T(8,128)S(1)} %copy-done.4, bf16[256,256]{1,0:T(8,128)(2,1)S(1)} %copy-done.5), custom_call_target="tpu_custom_call" | custom-call | tf_op jit(solution)/shard_map/spectra/pallas_call | solution.py:267
  86.8 4.7 %all-to-all-start.2 = ((f32[16,128,128]{2,1,0:T(8,128)}), f32[16,128,128]{2,1,0:T(8,128)S(1)}, u32[]{:S(2)}, u32[]{:S(2)}) async-start(f32[16,128,128]{2,1,0:T(8,128)} %bitcast.3), calls=%async_computation.2 | async-start | bytes 2097152 | tf_op jit(solution)/shard_map/all_to_all | solution.py:275
  91.5 17.2 %all-to-all-done.2 = f32[16,128,128]{2,1,0:T(8,128)S(1)} async-done(((f32[16,128,128]{2,1,0:T(8,128)}), f32[16,128,128]{2,1,0:T(8,128)S(1)}, u32[]{:S(2)}, u32[]{:S(2)}) %all-to-all-start.2) | async-done | bytes 1048608 | tf_op jit(solution)/shard_map/all_to_all | solution.py:275
  108.7 1.6 %order.1 = f32[8,256,128]{2,1,0:T(8,128)} custom-call(s32[1]{0:T(128)} %bitcast.first_ref, f32[2048,128]{1,0:T(8,128)S(1)} %bitcast.8), custom_call_target="tpu_custom_call" | custom-call | tf_op jit(solution)/shard_map/order/pallas_call | solution.py:277
Async XLA Ops:
  0.0 39.4 %copy-start = (bf16[8,512,256]{2,1,0:T(8,128)(2,1)S(1)}, bf16[8,512,256]{2,1,0:T(8,128)(2,1)}, u32[]{:S(2)}) copy-start(bf16[8,512,256]{2,1,0:T(8,128)(2,1)} %constant.19.clone.w_ref) | copy-start | bytes 6291460
  0.9 4.9 %collective-permute-start = (s32[6,2,128]{2,1,0:T(2,128)S(1)}, s32[6,2,128]{2,1,0:T(2,128)S(1)}, u32[]{:S(2)}, u32[]{:S(2)}) collective-permute-start(s32[6,2,128]{2,1,0:T(2,128)S(1)} %get-tuple-element.6), channel_id=1, source_target_pairs={{0,16},{16,32},{32,48},{48,64},{64,80},{80,96},{96,112},{112,128},... | collective-permute-start | bytes 18440 | tf_op jit(solution)/shard_map/ppermute | solution.py:244
  5.0 4.9 %collective-permute-start.1 = (s32[6,2,128]{2,1,0:T(2,128)S(1)}, s32[6,2,128]{2,1,0:T(2,128)S(1)}, u32[]{:S(2)}, u32[]{:S(2)}) collective-permute-start(s32[6,2,128]{2,1,0:T(2,128)S(1)} %get-tuple-element.5), channel_id=1, source_target_pairs={{16,0},{32,16},{48,32},{64,48},{80,64},{96,80},{112,96},{128,112},... | collective-permute-start | bytes 18440 | tf_op jit(solution)/shard_map/ppermute | solution.py:245
  9.9 1.1 %copy-start.1 = (s32[6,256,128]{2,1,0:T(8,128)S(1)}, s32[6,256,128]{2,1,0:T(8,128)}, u32[]{:S(2)}) copy-start(s32[6,256,128]{2,1,0:T(8,128)} %lab_ref.1) | copy-start | bytes 2359300
  11.0 0.7 copy-start.6
  39.4 40.8 %copy-start.2 = (bf16[1024,256]{1,0:T(8,128)(2,1)S(1)}, bf16[1024,256]{1,0:T(8,128)(2,1)}, u32[]{:S(2)}) copy-start(bf16[1024,256]{1,0:T(8,128)(2,1)} %constant.20.clone.y_ref) | copy-start | bytes 1572868
  39.4 40.8 %copy-start.3 = (f32[256,128]{1,0:T(8,128)S(1)}, f32[256,128]{1,0:T(8,128)}, u32[]{:S(2)}) copy-start(f32[256,128]{1,0:T(8,128)} %constant.21.clone.tr_ref) | copy-start | bytes 393220
  39.4 40.8 %copy-start.4 = (f32[256,128]{1,0:T(8,128)S(1)}, f32[256,128]{1,0:T(8,128)}, u32[]{:S(2)}) copy-start(f32[256,128]{1,0:T(8,128)} %constant.22.clone.ti_ref) | copy-start | bytes 393220
  39.4 40.8 %copy-start.5 = (bf16[256,256]{1,0:T(8,128)(2,1)S(1)}, bf16[256,256]{1,0:T(8,128)(2,1)}, u32[]{:S(2)}) copy-start(bf16[256,256]{1,0:T(8,128)(2,1)} %constant.23.clone.last_ref) | copy-start | bytes 393220
  86.8 21.9 %all-to-all-start.2 = ((f32[16,128,128]{2,1,0:T(8,128)}), f32[16,128,128]{2,1,0:T(8,128)S(1)}, u32[]{:S(2)}, u32[]{:S(2)}) async-start(f32[16,128,128]{2,1,0:T(8,128)} %bitcast.3), calls=%async_computation.2 | async-start | bytes 2097152 | tf_op jit(solution)/shard_map/all_to_all | solution.py:275

commit v2 on v1

--- a/solution.py
+++ b/solution.py
@@ -53,17 +53,21 @@
     return np.stack(entries)
 
 
+def joined(matrix, axis):
+    high, low = halves(matrix)
+    return np.concatenate([high, low, high], axis=axis)
+
+
 def y_matrix():
-    m = np.arange(256)[:, None]
-    i = np.arange(256)[None, :]
-    theta = 2.0 * math.pi / 256 * ((m * i) % 256)
-    high, low = halves(np.concatenate([np.cos(theta), np.sin(theta)], axis=0))
-    return np.concatenate([high, low], axis=0)
+    i = np.arange(256)[:, None]
+    m = np.arange(256)[None, :]
+    theta = 2.0 * math.pi / 256 * ((i * m) % 256)
+    return joined(np.concatenate([np.cos(theta), np.sin(theta)], axis=1), 0)
 
 
 def twiddles():
-    m = np.arange(256)[:, None]
-    r = np.arange(128)[None, :] % 16
+    r = np.arange(128)[:, None] % 16
+    m = np.arange(256)[None, :]
     phi = 2.0 * math.pi / 4096 * (m * r)
     return np.cos(phi).astype(np.float32), (-np.sin(phi)).astype(np.float32)
 
@@ -84,38 +88,57 @@
             w[2 * field + 1, plane, :, 1, 0, field, plane] = -cos
             w[2 * field + 1, plane, :, 0, 0, field, plane] = -sin
             w[2 * field + 1, plane, :, 1, 1, field, plane] = -sin
-    high, low = halves(w.reshape(128, 256))
-    return np.concatenate([high, low], axis=0)
-
-
-def rows_kernel(por_ref, lab_ref, up_ref, down_ref, out_ref, ext):
+    return joined(w.reshape(128, 256), 1)
+
+
+def along_x(por_ref, labels):
     def fill(ids):
         value = jnp.full(ids.shape, por_ref[0], jnp.float32)
         for k in range(1, 6):
             value = jnp.where(ids == k, por_ref[k], value)
         return value
 
-    def along_x(ref):
-        f = [fill(ref[x]) for x in range(6)]
-        s = [(f[k] + 6.0 * f[k + 1] + f[k + 2]) * 0.125 for k in range(4)]
-        return [s[2] - s[0], s[3] - s[1], s[1], s[2]]
-
-    for a, value in enumerate(along_x(lab_ref)):
-        ext[a, 8:264, :] = value
-    for a, value in enumerate(along_x(up_ref)):
-        ext[a, 6:8, :] = value
-    for a, value in enumerate(along_x(down_ref)):
-        ext[a, 264:266, :] = value
+    f = [fill(ids) for ids in labels]
+    s = [(f[k] + 6.0 * f[k + 1] + f[k + 2]) * 0.125 for k in range(4)]
+    return [s[2] - s[0], s[3] - s[1], s[1], s[2]]
+
+
+BLOCKS = 4
+TALL = 256 // BLOCKS
+
+
+def planes_kernel(por_ref, lab_ref, out_ref, held, sems):
+    copies = []
+    for b in range(BLOCKS):
+        rows = pl.ds(TALL * b, TALL)
+        copies.append(pltpu.make_async_copy(lab_ref.at[:, rows, :], held.at[:, rows, :], sems.at[b]))
+        copies[-1].start()
+    for b in range(BLOCKS):
+        copies[b].wait()
+        rows = pl.ds(TALL * b, TALL)
+        for a, value in enumerate(along_x(por_ref, [held[x, rows, :] for x in range(6)])):
+            out_ref[a, rows, :] = value
+
+
+def rows_kernel(por_ref, in_ref, next_ref, out_ref, ext):
+    ext[:, 0:256, :] = in_ref[...]
+    for a, value in enumerate(along_x(por_ref, [next_ref[x] for x in range(6)])):
+        ext[a, 256:260, :] = value
+
+    def along_y(a, first, count):
+        return (
+            ext[a, first - 1 : first - 1 + count, :]
+            + 6.0 * ext[a, first : first + count, :]
+            + ext[a, first + 1 : first + 1 + count, :]
+        ) * 0.125
+
     for a in range(4):
-        main = (ext[a, 7:263, :] + 6.0 * ext[a, 8:264, :] + ext[a, 9:265, :]) * 0.125
-        out_ref[:, 16 * a : 16 * a + 16, :] = main.reshape(16, 16, 128)
+        out_ref[:, 16 * a : 16 * a + 16, :] = along_y(a, 2, 256).reshape(16, 16, 128)
     for p in range(2):
         a = 2 + p
-        first = (ext[a, 6:7, :] + 6.0 * ext[a, 7:8, :] + ext[a, 8:9, :]) * 0.125
-        last = (ext[a, 263:264, :] + 6.0 * ext[a, 264:265, :] + ext[a, 265:266, :]) * 0.125
         for d in range(16):
-            below = first if d == 0 else out_ref[d - 1, 16 * a + 15 : 16 * a + 16, :]
-            above = last if d == 15 else out_ref[d + 1, 16 * a : 16 * a + 1, :]
+            below = along_y(a, 1, 1) if d == 0 else out_ref[d - 1, 16 * a + 15 : 16 * a + 16, :]
+            above = along_y(a, 258, 1) if d == 15 else out_ref[d + 1, 16 * a : 16 * a + 1, :]
             out_ref[d, 64 + 2 * p : 65 + 2 * p, :] = below
             out_ref[d, 65 + 2 * p : 66 + 2 * p, :] = above
     out_ref[:, 68:72, :] = jnp.zeros((16, 4, 128), jnp.float32)
@@ -195,44 +218,55 @@
         out_ref[16 - k] = both[128:] * sign
 
 
-def spectra_kernel(in_ref, y_ref, tr_ref, ti_ref, last_ref, out_ref):
+def modes_kernel(in_ref, y_ref, tr_ref, ti_ref, last_ref, out_ref):
+    tr, ti = tr_ref[...], ti_ref[...]
+    for pair in range(4):
+        turned = jnp.concatenate([in_ref[pl.ds(2 * pair + h, 256, stride=8), :].T for h in range(2)], axis=0)
+        high, low = split(turned)
+        both = dot(jnp.concatenate([high, high, low], axis=1), y_ref[...])
+        for h in range(2):
+            q = 2 * pair + h
+            cos, sin = both[128 * h : 128 * h + 128, :256], both[128 * h : 128 * h + 128, 256:]
+            high, low = split(jnp.concatenate([cos * tr + sin * ti, sin * tr - cos * ti], axis=0))
+            modes = dot(last_ref[...], jnp.concatenate([high, high, low], axis=0))
+            sr, si, pr, pi = modes[:32], modes[32:64], modes[64:96], modes[96:]
+            square = sr * sr + si * si
+            some = square > 1e-30
+            scale = lax.rsqrt(jnp.maximum(square, 1e-30))
+            results = (
+                square * scale,
+                jnp.where(some, (sr * pr + si * pi) * scale, jnp.sqrt(pr * pr + pi * pi)),
+                jnp.where(some, (si * pr - sr * pi) * scale, 0.0),
+            )
+            for o, result in enumerate(results):
+                for p in range(2):
+                    for half in range(2):
+                        block = result[16 * p : 16 * p + 16, 128 * half : 128 * half + 128]
+                        out_ref[pl.ds(place(o, p, half, q), 16, stride=96), :] = block
+
+
+def place(o, p, half, q):
+    return 32 * o + 16 * p + 8 * half + q
+
+
+def spectra_kernel(in_ref, out_ref):
     factor = 64.0 / (4096 * 2048)
-    for q in range(8):
-        high, low = split(in_ref[pl.ds(q, 256, stride=8), :])
-        main = dot(y_ref[...], high)
-        both = main[:512] + main[512:] + dot(y_ref[:512, :], low)
-        cos, sin = both[:256], both[256:]
-        tr, ti = tr_ref[...], ti_ref[...]
-        mixed = jnp.concatenate([cos * tr + sin * ti, sin * tr - cos * ti], axis=1)
-        high, low = split(mixed)
-        main = dot_t(last_ref[...], high)
-        modes = main[:128] + main[128:] + dot_t(last_ref[:128, :], low)
-        sr, si, pr, pi = modes[:32], modes[32:64], modes[64:96], modes[96:]
-        results = (
-            (sr * sr + si * si) * factor,
-            (pr * pr + pi * pi) * factor,
-            (sr * pr + si * pi) * factor,
-            (si * pr - sr * pi) * factor,
-        )
-        for o, result in enumerate(results):
-            for p in range(2):
-                for half in range(2):
-                    start = 8 * (2 * q + half) + 2 * o + p
-                    block = result[16 * p : 16 * p + 16, 128 * half : 128 * half + 128]
-                    out_ref[pl.ds(start, 16, stride=128), :] = block
-
-
-def order_kernel(first_ref, in_ref, out_ref):
     row = lax.broadcasted_iota(jnp.int32, (128, 128), 0)
     col = lax.broadcasted_iota(jnp.int32, (128, 128), 1)
-    drop = jnp.logical_and(row + col == 0, first_ref[0] == 1)
-    for o in range(8):
+    device = lax.axis_index("gy") + lax.axis_index("gz")
+    drop = row + col + device == 0
+    for p in range(2):
         for half in range(2):
-            parts = [in_ref[pl.ds(8 * (2 * q + half) + o, 16, stride=128), :] for q in range(8)]
-            block = jnp.concatenate(parts, axis=0).T
-            if half == 0:
-                block = jnp.where(drop, 0.0, block)
-            out_ref[o, 128 * half : 128 * half + 128, :] = block
+            size, re, im = [
+                jnp.concatenate([in_ref[pl.ds(place(o, p, half, q), 16, stride=96), :] for q in range(8)], axis=0).T
+                for o in range(3)
+            ]
+            scaled = size * factor
+            results = (size * scaled, (re * re + im * im) * factor, scaled * re, scaled * im)
+            for o, result in enumerate(results):
+                if half == 0:
+                    result = jnp.where(drop, 0.0, result)
+                out_ref[o, p, 128 * half : 128 * half + 128, :] = result
 
 
 def shape(*sizes):
@@ -241,17 +275,26 @@
 
 def shards(labels, porosity):
     count = lax.axis_size("gy")
-    up = lax.ppermute(labels[:, -2:, :], "gy", [(i, (i + 1) % count) for i in range(count)])
-    down = lax.ppermute(labels[:, :2, :], "gy", [((i + 1) % count, i) for i in range(count)])
+    following = lax.ppermute(labels[:, :4, :], "gy", [((i + 1) % count, i) for i in range(count)])
+    planes = pl.pallas_call(
+        planes_kernel,
+        out_shape=shape(4, 256, 128),
+        in_specs=[SMEM, pl.BlockSpec(memory_space=pl.ANY)],
+        out_specs=VMEM,
+        scratch_shapes=[pltpu.VMEM((6, 256, 128), jnp.int32), pltpu.SemaphoreType.DMA((BLOCKS,))],
+        compiler_params=PARAMS,
+        cost_estimate=pl.CostEstimate(flops=10_000_000, bytes_accessed=4_000_000, transcendentals=0),
+        name="planes",
+    )(porosity, labels)
     rows = pl.pallas_call(
         rows_kernel,
         out_shape=shape(16, 72, 128),
-        in_specs=[SMEM, VMEM, VMEM, VMEM],
-        out_specs=VMEM,
-        scratch_shapes=[pltpu.VMEM((4, 272, 128), jnp.float32)],
+        in_specs=[SMEM, VMEM, VMEM],
+        out_specs=VMEM,
+        scratch_shapes=[pltpu.VMEM((4, 264, 128), jnp.float32)],
         compiler_params=PARAMS,
         name="rows",
-    )(porosity, labels, up, down)
+    )(porosity, planes, following)
     rows = lax.all_to_all(rows, "gz", 0, 0, tiled=True)
     columns = pl.pallas_call(
         columns_kernel,
@@ -264,25 +307,23 @@
     )(rows, jnp.asarray(z_matrices()))
     columns = lax.all_to_all(columns.reshape(256, 8, 128), ("gy", "gz"), 0, 0, tiled=True)
     cos, sin = twiddles()
-    spectra = pl.pallas_call(
+    modes = pl.pallas_call(
+        modes_kernel,
+        out_shape=shape(16 * 96, 128),
+        in_specs=[VMEM] * 5,
+        out_specs=VMEM,
+        compiler_params=PARAMS,
+        name="modes",
+    )(columns.reshape(2048, 128), jnp.asarray(y_matrix()), jnp.asarray(cos), jnp.asarray(sin), jnp.asarray(last_matrix()))
+    modes = lax.all_to_all(modes.reshape(16, 96, 128), "gy", 0, 0, tiled=True)
+    return pl.pallas_call(
         spectra_kernel,
-        out_shape=shape(2048, 128),
-        in_specs=[VMEM] * 5,
+        out_shape=shape(4, 2, 256, 128),
+        in_specs=[VMEM],
         out_specs=VMEM,
         compiler_params=PARAMS,
         name="spectra",
-    )(columns.reshape(2048, 128), jnp.asarray(y_matrix()), jnp.asarray(cos), jnp.asarray(sin), jnp.asarray(last_matrix()))
-    spectra = lax.all_to_all(spectra.reshape(16, 128, 128), "gy", 0, 0, tiled=True)
-    origin = jnp.logical_and(lax.axis_index("gy") == 0, lax.axis_index("gz") == 0).astype(jnp.int32).reshape(1)
-    result = pl.pallas_call(
-        order_kernel,
-        out_shape=shape(8, 256, 128),
-        in_specs=[SMEM, VMEM],
-        out_specs=VMEM,
-        compiler_params=PARAMS,
-        name="order",
-    )(origin, spectra.reshape(2048, 128))
-    return result.reshape(4, 2, 256, 128)
+    )(modes.reshape(16 * 96, 128))
 
 
 def solution(mesh):

time: 111 us -> 101 us (0.910)
  waiting for transfers between devices: 22.1 us -> 0.01 us
  blocking collectives: 65.6 us -> 86.8 us
  starting transfers between devices: 8.84 us -> 3.24 us
  Pallas kernels: 11 us -> 7.6 us
    all_to_all x0 -> x1, blocking collectives: none -> 18.8 us  [shards(): modes = lax.all_to_all(modes.reshape(16, 96, 128), 'gy', 0, 0, tiled=True)]
    all_to_all x1 -> x0, waiting for transfers between devices: 17.2 us -> none  [shards(): lax.all_to_all(spectra.reshape(16, 128, 128), 'gy', 0, 0, tiled=True)]
    ppermute x2 -> x1, waiting for transfers between devices: 4.85 us -> 0.01 us  [shards(): lax.ppermute(labels[:, :4, :], 'gy', [((i + 1) % count, i) for i in range...]
    all_to_all x1 -> x0, starting transfers between devices: 4.7 us -> none  [shards(): lax.all_to_all(spectra.reshape(16, 128, 128), 'gy', 0, 0, tiled=True)]
    all_to_all x1, blocking collectives: 39 us -> 43.6 us  [shards(): lax.all_to_all(columns.reshape(256, 8, 128), ('gy', 'gz'), 0, 0, tiled=True)]
    pallas_call x2 -> x3, Pallas kernels: 8.24 us -> 5.17 us  [the longest x1 2.53 us: shards(): pl.pallas_call(modes_kernel, out_shape=shape(16 * 96, 128), in_specs=[VME...]
    all_to_all x1, blocking collectives: 26.6 us -> 24.4 us  [shards(): rows = lax.all_to_all(rows, 'gz', 0, 0, tiled=True)]
    ppermute x2 -> x1, starting transfers between devices: 4.14 us -> 3.24 us  [shards(): lax.ppermute(labels[:, :4, :], 'gy', [((i + 1) % count, i) for i in range...]
  transfers between devices with their start and end apart: 3 -> 1, of which waited for: 3 -> 0; matrix products, arithmetic and copies ran while one was open for 0% -> 0% of each run, Pallas kernels for 0% -> 1%
where the time goes in v2:
time: 101 us; the launch traced here: 100 us
  blocking collectives  86.8 us (86%)
  Pallas kernels  7.6 us (8%)
  starting transfers between devices  3.24 us (3%)
  local copies, waits for them, and re-layouts  2.7 us (3%)
    all_to_all x1, blocking collectives, shards(): lax.all_to_all(columns.reshape(256, 8, 128), ('gy', 'gz'), 0, 0, tiled=True)  43.6 us
    all_to_all x1, blocking collectives, shards(): rows = lax.all_to_all(rows, 'gz', 0, 0, tiled=True)  24.4 us
    all_to_all x1, blocking collectives, shards(): modes = lax.all_to_all(modes.reshape(16, 96, 128), 'gy', 0, 0, tiled=True)  18.8 us
    ppermute x1, starting transfers between devices, shards(): lax.ppermute(labels[:, :4, :], 'gy', [((i + 1) % count, i) for i in range...  3.24 us
    pallas_call x1, Pallas kernels, shards(): pl.pallas_call(modes_kernel, out_shape=shape(16 * 96, 128), in_specs=[VME...  2.53 us
  transfers between devices with their start and end apart: 1, of which 0 were waited for; matrix products, arithmetic and copies ran while one was open for 0% of the time, Pallas kernels for 1%

profile of v2, /device:TPU:1, one launch (start us, length us, event | category | flops | bytes accessed | tf_op | source)
XLA Modules:
  0.0 100.4 jit_solution(2341168390995042027)
XLA Ops:
  0.0 0.0 copy-start
  0.0 0.9 slice.3
  0.9 3.2 %collective-permute-start = (s32[6,4,128]{2,1,0:T(4,128)S(1)}, s32[6,4,128]{2,1,0:T(4,128)S(1)}, u32[]{:S(2)}, u32[]{:S(2)}) collective-permute-start(s32[6,4,128]{2,1,0:T(4,128)S(1)} %slice.3), channel_id=1, source_target_pairs={{16,0},{32,16},{48,32},{64,48},{80,64},{96,80},{112,96},{128,112},... | collective-permute-start | bytes 36872 | tf_op jit(solution)/shard_map/ppermute | solution.py:278
  4.1 0.0 copy-start.1
  4.1 1.1 %copy-done.1 = s32[6,256,128]{2,1,0:T(8,128)S(1)} copy-done((s32[6,256,128]{2,1,0:T(8,128)S(1)}, s32[6,256,128]{2,1,0:T(8,128)}, u32[]{:S(2)}) %copy-start.1) | copy-done | bytes 786456
  5.3 0.0 copy-start.6
  5.3 0.7 copy-done.6
  5.9 1.1 %planes.1.in_ref = f32[4,256,128]{2,1,0:T(8,128)S(1)} custom-call(f32[6]{0:T(128)S(1)} %copy-done.6, s32[6,256,128]{2,1,0:T(8,128)S(1)} %copy-done.1), custom_call_target="tpu_custom_call" | custom-call | flops 10000000 | bytes 4000000 | tf_op jit(solution)/shard_map/planes/pallas_call | solution.py:279
  7.0 0.0 collective-permute-done.next_ref
  7.0 0.7 rows.1
  7.8 24.4 %all_to_all.15.in_ref = f32[16,72,128]{2,1,0:T(8,128)S(1)} all-to-all(f32[16,72,128]{2,1,0:T(8,128)S(1)} %rows.1), channel_id=1, replica_groups=mesh['gy'=16,'gz'=16] {'gz'}, dimensions={0} | all-to-all | bytes 1179648 | tf_op jit(solution)/shard_map/all_to_all | solution.py:298
  32.2 0.0 copy-done
  32.2 0.0 copy-start.2
  32.2 0.0 copy-start.3
  32.2 0.0 copy-start.4
  32.2 0.0 copy-start.5
  32.2 1.7 %columns.1 = f32[16,128,128]{2,1,0:T(8,128)S(1)} custom-call(f32[16,72,128]{2,1,0:T(8,128)S(1)} %all_to_all.15.in_ref, bf16[8,512,256]{2,1,0:T(8,128)(2,1)S(1)} %copy-done), custom_call_target="tpu_custom_call" | custom-call | tf_op jit(solution)/shard_map/columns/pallas_call | solution.py:299
  33.9 43.6 %all_to_all.16 = f32[256,8,128]{2,1,0:T(8,128)S(1)} all-to-all(f32[256,8,128]{2,1,0:T(8,128)S(1)} %bitcast.5), channel_id=1, replica_groups=mesh['gy'=16,'gz'=16] {'gy','gz'}, dimensions={0} | all-to-all | bytes 2097152 | tf_op jit(solution)/shard_map/all_to_all | solution.py:308
  77.5 0.0 copy-done.2
  77.5 0.0 copy-done.3
  77.5 0.0 copy-done.4
  77.5 0.0 copy-done.5
  77.5 2.5 %modes.1 = f32[1536,128]{1,0:T(8,128)S(1)} custom-call(f32[2048,128]{1,0:T(8,128)S(1)} %bitcast.4, bf16[768,512]{1,0:T(8,128)(2,1)S(1)} %copy-done.2, f32[128,256]{1,0:T(8,128)S(1)} %copy-done.5, f32[128,256]{1,0:T(8,128)S(1)} %copy-done.4, bf16[128,768]{1,0:T(8,128)(2,1)S(1)} %copy-done.3), custom_call_target="tpu_custom_call" | custom-call | tf_op jit(solution)/shard_map/modes/pallas_call | solution.py:310
  80.0 18.8 %all_to_all.17 = f32[16,96,128]{2,1,0:T(8,128)S(1)} all-to-all(f32[16,96,128]{2,1,0:T(8,128)S(1)} %bitcast.7), channel_id=1, replica_groups=mesh['gy'=16,'gz'=16] {'gy'}, dimensions={0} | all-to-all | bytes 1572864 | tf_op jit(solution)/shard_map/all_to_all | solution.py:318
  98.8 1.5 %spectra.1 = f32[4,2,256,128]{3,2,1,0:T(8,128)} custom-call(f32[1536,128]{1,0:T(8,128)S(1)} %bitcast.6), custom_call_target="tpu_custom_call" | custom-call | tf_op jit(solution)/shard_map/spectra/pallas_call | solution.py:319
Async XLA Ops:
  0.0 32.2 %copy-start = (bf16[8,512,256]{2,1,0:T(8,128)(2,1)S(1)}, bf16[8,512,256]{2,1,0:T(8,128)(2,1)}, u32[]{:S(2)}) copy-start(bf16[8,512,256]{2,1,0:T(8,128)(2,1)} %constant.10.clone.w_ref) | copy-start | bytes 6291460
  0.9 6.1 %collective-permute-start = (s32[6,4,128]{2,1,0:T(4,128)S(1)}, s32[6,4,128]{2,1,0:T(4,128)S(1)}, u32[]{:S(2)}, u32[]{:S(2)}) collective-permute-start(s32[6,4,128]{2,1,0:T(4,128)S(1)} %slice.3), channel_id=1, source_target_pairs={{16,0},{32,16},{48,32},{64,48},{80,64},{96,80},{112,96},{128,112},... | collective-permute-start | bytes 36872 | tf_op jit(solution)/shard_map/ppermute | solution.py:278
  4.1 1.1 %copy-start.1 = (s32[6,256,128]{2,1,0:T(8,128)S(1)}, s32[6,256,128]{2,1,0:T(8,128)}, u32[]{:S(2)}) copy-start(s32[6,256,128]{2,1,0:T(8,128)} %lab_ref.1) | copy-start | bytes 2359300
  5.3 0.7 copy-start.6
  32.2 45.3 %copy-start.2 = (bf16[768,512]{1,0:T(8,128)(2,1)S(1)}, bf16[768,512]{1,0:T(8,128)(2,1)}, u32[]{:S(2)}) copy-start(bf16[768,512]{1,0:T(8,128)(2,1)} %constant.11.clone.y_ref) | copy-start | bytes 2359300
  32.2 45.3 %copy-start.3 = (bf16[128,768]{1,0:T(8,128)(2,1)S(1)}, bf16[128,768]{1,0:T(8,128)(2,1)}, u32[]{:S(2)}) copy-start(bf16[128,768]{1,0:T(8,128)(2,1)} %constant.14.clone.last_ref) | copy-start | bytes 589828
  32.2 45.3 %copy-start.4 = (f32[128,256]{1,0:T(8,128)S(1)}, f32[128,256]{1,0:T(8,128)}, u32[]{:S(2)}) copy-start(f32[128,256]{1,0:T(8,128)} %constant.13.clone.ti_ref) | copy-start | bytes 393220
  32.2 45.3 %copy-start.5 = (f32[128,256]{1,0:T(8,128)S(1)}, f32[128,256]{1,0:T(8,128)}, u32[]{:S(2)}) copy-start(f32[128,256]{1,0:T(8,128)} %constant.12.clone.tr_ref) | copy-start | bytes 393220

commit v3 on v2

--- a/solution.py
+++ b/solution.py
@@ -11,7 +11,8 @@
 from jax.sharding import PartitionSpec as P
 
 VMEM = pl.BlockSpec(memory_space=pltpu.VMEM)
-SMEM = pl.BlockSpec(memory_space=pltpu.SMEM)
+HBM = pl.BlockSpec(memory_space=pltpu.HBM)
+WIDE = pltpu.CompilerParams(vmem_limit_bytes=54000 * 1024)
 PARAMS = pltpu.CompilerParams(vmem_limit_bytes=48 * 1024 * 1024)
 
 
@@ -35,6 +36,11 @@
     return lax.dot_general(a, b, (((1,), (1,)), ((), ())), preferred_element_type=jnp.float32)
 
 
+def joined(matrix, axis):
+    high, low = halves(matrix)
+    return np.concatenate([high, low, high], axis=axis)
+
+
 def z_matrices():
     q = np.arange(128)[:, None]
     j = np.arange(128)[None, :]
@@ -43,19 +49,8 @@
         theta = 2.0 * math.pi / 2048 * ((j * (16 * q + s)) % 2048)
         return np.concatenate([np.cos(theta), sign * np.sin(theta)], axis=1)
 
-    entries = []
-    for e in range(8):
-        first = block(e, 1.0)
-        second = block(8, 1.0) if e == 0 else block(16 - e, -1.0)
-        high_a, low_a = halves(first)
-        high_b, low_b = halves(second)
-        entries.append(np.concatenate([high_a, high_b, low_a, low_b], axis=0))
-    return np.stack(entries)
-
-
-def joined(matrix, axis):
-    high, low = halves(matrix)
-    return np.concatenate([high, low, high], axis=axis)
+    pairs = [(block(0, 1.0), block(8, 1.0))] + [(block(s, 1.0), block(16 - s, -1.0)) for s in range(1, 8)]
+    return np.stack([joined(np.concatenate(pair, axis=0), 1) for pair in pairs])
 
 
 def y_matrix():
@@ -91,11 +86,11 @@
     return joined(w.reshape(128, 256), 1)
 
 
-def along_x(por_ref, labels):
+def along_x(values, labels):
     def fill(ids):
-        value = jnp.full(ids.shape, por_ref[0], jnp.float32)
-        for k in range(1, 6):
-            value = jnp.where(ids == k, por_ref[k], value)
+        value = jnp.where(ids == 1, values[1], values[0])
+        for k in range(2, 6):
+            value = jnp.where(ids == k, values[k], value)
         return value
 
     f = [fill(ids) for ids in labels]
@@ -103,45 +98,65 @@
     return [s[2] - s[0], s[3] - s[1], s[1], s[2]]
 
 
+def along_y(ext, a, first, count):
+    return (
+        ext[a, first + 1 : first + 1 + count, :]
+        + 6.0 * ext[a, first + 2 : first + 2 + count, :]
+        + ext[a, first + 3 : first + 3 + count, :]
+    ) * 0.125
+
+
 BLOCKS = 4
 TALL = 256 // BLOCKS
 
 
-def planes_kernel(por_ref, lab_ref, out_ref, held, sems):
-    copies = []
+def planes_kernel(por_ref, lab_ref, out_ref, end_ref, table_ref, held, few, ext, sems):
+    copies = [pltpu.make_async_copy(por_ref, few, sems.at[BLOCKS])]
     for b in range(BLOCKS):
         rows = pl.ds(TALL * b, TALL)
         copies.append(pltpu.make_async_copy(lab_ref.at[:, rows, :], held.at[:, rows, :], sems.at[b]))
-        copies[-1].start()
+    for copy in copies:
+        copy.start()
+    copies[0].wait()
+    values = [few[k] for k in range(6)]
+    for k in range(6):
+        table_ref[k : k + 1, :] = jnp.full((1, 128), values[k], jnp.float32)
+    table_ref[6:8, :] = jnp.zeros((2, 128), jnp.float32)
+    done = 0
     for b in range(BLOCKS):
-        copies[b].wait()
+        copies[1 + b].wait()
         rows = pl.ds(TALL * b, TALL)
-        for a, value in enumerate(along_x(por_ref, [held[x, rows, :] for x in range(6)])):
-            out_ref[a, rows, :] = value
-
-
-def rows_kernel(por_ref, in_ref, next_ref, out_ref, ext):
-    ext[:, 0:256, :] = in_ref[...]
-    for a, value in enumerate(along_x(por_ref, [next_ref[x] for x in range(6)])):
-        ext[a, 256:260, :] = value
-
-    def along_y(a, first, count):
-        return (
-            ext[a, first - 1 : first - 1 + count, :]
-            + 6.0 * ext[a, first : first + count, :]
-            + ext[a, first + 1 : first + 1 + count, :]
-        ) * 0.125
-
-    for a in range(4):
-        out_ref[:, 16 * a : 16 * a + 16, :] = along_y(a, 2, 256).reshape(16, 16, 128)
+        for a, value in enumerate(along_x(values, [held[x, rows, :] for x in range(6)])):
+            ext[a, rows, :] = value
+        ready = (TALL * (b + 1) - 3) // 16
+        for a in range(4):
+            block = along_y(ext, a, 16 * done, 16 * (ready - done))
+            out_ref[done:ready, 16 * a : 16 * a + 16, :] = block.reshape(ready - done, 16, 128)
+        done = ready
     for p in range(2):
         a = 2 + p
-        for d in range(16):
-            below = along_y(a, 1, 1) if d == 0 else out_ref[d - 1, 16 * a + 15 : 16 * a + 16, :]
-            above = along_y(a, 258, 1) if d == 15 else out_ref[d + 1, 16 * a : 16 * a + 1, :]
+        for d in range(15):
+            below = along_y(ext, a, -1, 1) if d == 0 else out_ref[d - 1, 16 * a + 15 : 16 * a + 16, :]
+            above = along_y(ext, a, 240, 1) if d == 14 else out_ref[d + 1, 16 * a : 16 * a + 1, :]
             out_ref[d, 64 + 2 * p : 65 + 2 * p, :] = below
             out_ref[d, 65 + 2 * p : 66 + 2 * p, :] = above
-    out_ref[:, 68:72, :] = jnp.zeros((16, 4, 128), jnp.float32)
+    out_ref[0:15, 68:72, :] = jnp.zeros((15, 4, 128), jnp.float32)
+    out_ref[15] = jnp.zeros((72, 128), jnp.float32)
+    end_ref[...] = ext[:, 232:256, :]
+
+
+def rows_kernel(in_ref, end_ref, table_ref, next_ref, out_ref, ext):
+    out_ref[0:15] = in_ref[0:15]
+    ext[:, 0:24, :] = end_ref[...]
+    values = [table_ref[k : k + 1, :] for k in range(6)]
+    for a, value in enumerate(along_x(values, [next_ref[x] for x in range(6)])):
+        ext[a, 24:28, :] = value
+        out_ref[15, 16 * a : 16 * a + 16, :] = along_y(ext, a, 8, 16)
+    for p in range(2):
+        a = 2 + p
+        out_ref[15, 64 + 2 * p : 65 + 2 * p, :] = along_y(ext, a, 7, 1)
+        out_ref[15, 65 + 2 * p : 66 + 2 * p, :] = along_y(ext, a, 24, 1)
+    out_ref[15, 68:72, :] = jnp.zeros((4, 128), jnp.float32)
 
 
 def real_transform(x):
@@ -202,61 +217,56 @@
             im = jnp.zeros_like(re)
         top = jnp.concatenate([re, im], axis=1)
         bottom = jnp.concatenate([im, -re], axis=1)
-        return split(jnp.concatenate([top, bottom], axis=0))
-
-    for k in (0, 8):
-        high, low = arranged(k)
-        at = 16 * k
-        lead = w_ref[0, at : at + 128, :]
-        tail = w_ref[0, at + 256 : at + 384, :]
-        out_ref[k] = dot_t(lead, high) + dot_t(tail, high) + dot_t(lead, low)
+        high, low = split(jnp.concatenate([top, bottom], axis=0))
+        return jnp.concatenate([high, high, low], axis=1)
+
+    out_ref[0] = dot_t(w_ref[0, :128, :], arranged(0))
+    out_ref[8] = dot_t(w_ref[0, 128:, :], arranged(8))
     for k in range(1, 8):
-        high, low = arranged(k)
-        main = dot_t(w_ref[k], high)
-        both = main[:256] + main[256:] + dot_t(w_ref[k, :256, :], low)
+        both = dot_t(w_ref[k], arranged(k))
         out_ref[k] = both[:128]
         out_ref[16 - k] = both[128:] * sign
 
 
 def modes_kernel(in_ref, y_ref, tr_ref, ti_ref, last_ref, out_ref):
     tr, ti = tr_ref[...], ti_ref[...]
-    for pair in range(4):
-        turned = jnp.concatenate([in_ref[pl.ds(2 * pair + h, 256, stride=8), :].T for h in range(2)], axis=0)
-        high, low = split(turned)
-        both = dot(jnp.concatenate([high, high, low], axis=1), y_ref[...])
-        for h in range(2):
-            q = 2 * pair + h
-            cos, sin = both[128 * h : 128 * h + 128, :256], both[128 * h : 128 * h + 128, 256:]
-            high, low = split(jnp.concatenate([cos * tr + sin * ti, sin * tr - cos * ti], axis=0))
-            modes = dot(last_ref[...], jnp.concatenate([high, high, low], axis=0))
-            sr, si, pr, pi = modes[:32], modes[32:64], modes[64:96], modes[96:]
-            square = sr * sr + si * si
-            some = square > 1e-30
-            scale = lax.rsqrt(jnp.maximum(square, 1e-30))
-            results = (
-                square * scale,
-                jnp.where(some, (sr * pr + si * pi) * scale, jnp.sqrt(pr * pr + pi * pi)),
-                jnp.where(some, (si * pr - sr * pi) * scale, 0.0),
-            )
-            for o, result in enumerate(results):
-                for p in range(2):
-                    for half in range(2):
-                        block = result[16 * p : 16 * p + 16, 128 * half : 128 * half + 128]
-                        out_ref[pl.ds(place(o, p, half, q), 16, stride=96), :] = block
+    turned = jnp.concatenate([in_ref[pl.ds(q, 256, stride=8), :].T for q in range(8)], axis=0)
+    high, low = split(turned)
+    both = dot(jnp.concatenate([high, high, low], axis=1), y_ref[...])
+    for q in range(8):
+        cos, sin = both[128 * q : 128 * q + 128, :256], both[128 * q : 128 * q + 128, 256:]
+        high, low = split(jnp.concatenate([cos * tr + sin * ti, sin * tr - cos * ti], axis=0))
+        modes = dot(last_ref[...], jnp.concatenate([high, high, low], axis=0))
+        sr, si, pr, pi = modes[:32], modes[32:64], modes[64:96], modes[96:]
+        square = sr * sr + si * si
+        some = square > 1e-30
+        scale = lax.rsqrt(jnp.maximum(square, 1e-30))
+        results = (
+            square * scale,
+            jnp.where(some, (sr * pr + si * pi) * scale, jnp.sqrt(pr * pr + pi * pi)),
+            jnp.where(some, (si * pr - sr * pi) * scale, 0.0),
+        )
+        for o, result in enumerate(results):
+            for p in range(2):
+                for half in range(2):
+                    block = result[16 * p : 16 * p + 16, 128 * half : 128 * half + 128]
+                    out_ref[pl.ds(place(o, p, half, q), 16, stride=96), :] = block
 
 
 def place(o, p, half, q):
     return 32 * o + 16 * p + 8 * half + q
 
 
-def spectra_kernel(in_ref, out_ref):
+def spectra_kernel(in_ref, out_ref, held, sems):
     factor = 64.0 / (4096 * 2048)
     row = lax.broadcasted_iota(jnp.int32, (128, 128), 0)
     col = lax.broadcasted_iota(jnp.int32, (128, 128), 1)
     device = lax.axis_index("gy") + lax.axis_index("gz")
     drop = row + col + device == 0
+    copies = []
     for p in range(2):
         for half in range(2):
+            at = 2 * p + half
             size, re, im = [
                 jnp.concatenate([in_ref[pl.ds(place(o, p, half, q), 16, stride=96), :] for q in range(8)], axis=0).T
                 for o in range(3)
@@ -264,9 +274,11 @@
             scaled = size * factor
             results = (size * scaled, (re * re + im * im) * factor, scaled * re, scaled * im)
             for o, result in enumerate(results):
-                if half == 0:
-                    result = jnp.where(drop, 0.0, result)
-                out_ref[o, p, 128 * half : 128 * half + 128, :] = result
+                held[at, o] = jnp.where(drop, 0.0, result) if half == 0 else result
+            copies.append(pltpu.make_async_copy(held.at[at], out_ref.at[:, p, pl.ds(128 * half, 128), :], sems.at[at]))
+            copies[-1].start()
+    for copy in copies:
+        copy.wait()
 
 
 def shape(*sizes):
@@ -276,25 +288,30 @@
 def shards(labels, porosity):
     count = lax.axis_size("gy")
     following = lax.ppermute(labels[:, :4, :], "gy", [((i + 1) % count, i) for i in range(count)])
-    planes = pl.pallas_call(
+    planes, ends, table = pl.pallas_call(
         planes_kernel,
-        out_shape=shape(4, 256, 128),
-        in_specs=[SMEM, pl.BlockSpec(memory_space=pl.ANY)],
-        out_specs=VMEM,
-        scratch_shapes=[pltpu.VMEM((6, 256, 128), jnp.int32), pltpu.SemaphoreType.DMA((BLOCKS,))],
-        compiler_params=PARAMS,
+        out_shape=(shape(16, 72, 128), shape(4, 24, 128), shape(8, 128)),
+        in_specs=[HBM, HBM],
+        out_specs=(VMEM, VMEM, VMEM),
+        scratch_shapes=[
+            pltpu.VMEM((6, 256, 128), jnp.int32),
+            pltpu.SMEM((6,), jnp.float32),
+            pltpu.VMEM((4, 256, 128), jnp.float32),
+            pltpu.SemaphoreType.DMA((BLOCKS + 1,)),
+        ],
+        compiler_params=WIDE,
         cost_estimate=pl.CostEstimate(flops=10_000_000, bytes_accessed=4_000_000, transcendentals=0),
         name="planes",
     )(porosity, labels)
     rows = pl.pallas_call(
         rows_kernel,
         out_shape=shape(16, 72, 128),
-        in_specs=[SMEM, VMEM, VMEM],
+        in_specs=[VMEM, VMEM, VMEM, VMEM],
         out_specs=VMEM,
-        scratch_shapes=[pltpu.VMEM((4, 264, 128), jnp.float32)],
+        scratch_shapes=[pltpu.VMEM((4, 32, 128), jnp.float32)],
         compiler_params=PARAMS,
         name="rows",
-    )(porosity, planes, following)
+    )(planes, ends, table, following)
     rows = lax.all_to_all(rows, "gz", 0, 0, tiled=True)
     columns = pl.pallas_call(
         columns_kernel,
@@ -320,7 +337,8 @@
         spectra_kernel,
         out_shape=shape(4, 2, 256, 128),
         in_specs=[VMEM],
-        out_specs=VMEM,
+        out_specs=HBM,
+        scratch_shapes=[pltpu.VMEM((4, 4, 128, 128), jnp.float32), pltpu.SemaphoreType.DMA((4,))],
         compiler_params=PARAMS,
         name="spectra",
     )(modes.reshape(16 * 96, 128))

time: 101 us -> 98.4 us (0.974)
  local copies, waits for them, and re-layouts: 2.7 us -> 1.57 us
    all_to_all x1, blocking collectives: 43.6 us -> 42.3 us  [shards(): lax.all_to_all(columns.reshape(256, 8, 128), ('gy', 'gz'), 0, 0, tiled=True)]
    unnamed x14 -> x12, local copies, waits for them, and re-layouts: 1.81 us -> 0.68 us
    all_to_all x1, blocking collectives: 24.4 us -> 25.5 us  [shards(): rows = lax.all_to_all(rows, 'gz', 0, 0, tiled=True)]
  transfers between devices with their start and end apart: 1 -> 1, of which waited for: 0 -> 1; matrix products, arithmetic and copies ran while one was open for 0% -> 0% of each run, Pallas kernels for 1% -> 1%
where the time goes in v3:
time: 98.4 us; the launch traced here: 98.2 us
  blocking collectives  86.6 us (88%)
  Pallas kernels  6.61 us (7%)
  starting transfers between devices  3.24 us (3%)
  local copies, waits for them, and re-layouts  1.57 us (2%)
    all_to_all x1, blocking collectives, shards(): lax.all_to_all(columns.reshape(256, 8, 128), ('gy', 'gz'), 0, 0, tiled=True)  42.3 us
    all_to_all x1, blocking collectives, shards(): rows = lax.all_to_all(rows, 'gz', 0, 0, tiled=True)  25.5 us
    all_to_all x1, blocking collectives, shards(): modes = lax.all_to_all(modes.reshape(16, 96, 128), 'gy', 0, 0, tiled=True)  18.8 us
    ppermute x1, starting transfers between devices, shards(): lax.ppermute(labels[:, :4, :], 'gy', [((i + 1) % count, i) for i in range...  3.24 us
    pallas_call x1, Pallas kernels, shards(): pl.pallas_call(modes_kernel, out_shape=shape(16 * 96, 128), in_specs=[VME...  2.04 us
  transfers between devices with their start and end apart: 1, of which 1 were waited for; matrix products, arithmetic and copies ran while one was open for 0% of the time, Pallas kernels for 1%

profile of v3, /device:TPU:1, one launch (start us, length us, event | category | flops | bytes accessed | tf_op | source)
XLA Modules:
  0.0 98.2 jit_solution(9911936378567998869)
XLA Ops:
  0.0 0.0 copy-start
  0.0 0.9 slice.3
  0.9 3.2 %collective-permute-start = (s32[6,4,128]{2,1,0:T(4,128)S(1)}, s32[6,4,128]{2,1,0:T(4,128)S(1)}, u32[]{:S(2)}, u32[]{:S(2)}) collective-permute-start(s32[6,4,128]{2,1,0:T(4,128)S(1)} %slice.3), channel_id=1, source_target_pairs={{16,0},{32,16},{48,32},{64,48},{80,64},{96,80},{112,96},{128,112},... | collective-permute-start | bytes 36872 | tf_op jit(solution)/shard_map/ppermute | solution.py:290
  4.1 0.0 copy-start.5
  4.1 0.7 copy-done.5
  4.8 1.4 %planes.1 = (f32[16,72,128]{2,1,0:T(8,128)S(1)}, f32[4,24,128]{2,1,0:T(8,128)S(1)}, f32[8,128]{1,0:T(8,128)S(1)}) custom-call(f32[6]{0:T(128)S(1)} %copy-done.5, s32[6,256,128]{2,1,0:T(8,128)} %lab_ref.1), custom_call_target="tpu_custom_call" | custom-call | flops 10000000 | bytes 4000000 | tf_op jit(solution)/shard_map/planes/pallas_call | solution.py:291
  6.2 0.2 collective-permute-done.next_ref
  6.4 0.1 rows.1
  6.5 25.5 %all_to_all.15.in_ref = f32[16,72,128]{2,1,0:T(8,128)S(1)} all-to-all(f32[16,72,128]{2,1,0:T(8,128)S(1)} %rows.1), channel_id=1, replica_groups=mesh['gy'=16,'gz'=16] {'gz'}, dimensions={0} | all-to-all | bytes 1179648 | tf_op jit(solution)/shard_map/all_to_all | solution.py:315
  31.9 0.0 copy-done
  32.0 0.0 copy-start.1
  32.0 0.0 copy-start.2
  32.0 0.0 copy-start.3
  32.0 0.0 copy-start.4
  32.0 1.7 %columns.1 = f32[16,128,128]{2,1,0:T(8,128)S(1)} custom-call(f32[16,72,128]{2,1,0:T(8,128)S(1)} %all_to_all.15.in_ref, bf16[8,256,768]{2,1,0:T(8,128)(2,1)S(1)} %copy-done), custom_call_target="tpu_custom_call" | custom-call | tf_op jit(solution)/shard_map/columns/pallas_call | solution.py:316
  33.7 42.3 %all_to_all.16 = f32[256,8,128]{2,1,0:T(8,128)S(1)} all-to-all(f32[256,8,128]{2,1,0:T(8,128)S(1)} %bitcast.5), channel_id=1, replica_groups=mesh['gy'=16,'gz'=16] {'gy','gz'}, dimensions={0} | all-to-all | bytes 2097152 | tf_op jit(solution)/shard_map/all_to_all | solution.py:325
  76.0 0.0 copy-done.1
  76.0 0.0 copy-done.2
  76.0 0.0 copy-done.3
  76.0 0.0 copy-done.4
  76.0 2.0 %modes.1 = f32[1536,128]{1,0:T(8,128)S(1)} custom-call(f32[2048,128]{1,0:T(8,128)S(1)} %bitcast.4, bf16[768,512]{1,0:T(8,128)(2,1)S(1)} %copy-done.1, f32[128,256]{1,0:T(8,128)S(1)} %copy-done.4, f32[128,256]{1,0:T(8,128)S(1)} %copy-done.3, bf16[128,768]{1,0:T(8,128)(2,1)S(1)} %copy-done.2), custom_call_target="tpu_custom_call" | custom-call | tf_op jit(solution)/shard_map/modes/pallas_call | solution.py:327
  78.1 18.8 %all_to_all.17 = f32[16,96,128]{2,1,0:T(8,128)S(1)} all-to-all(f32[16,96,128]{2,1,0:T(8,128)S(1)} %bitcast.7), channel_id=1, replica_groups=mesh['gy'=16,'gz'=16] {'gy'}, dimensions={0} | all-to-all | bytes 1572864 | tf_op jit(solution)/shard_map/all_to_all | solution.py:335
  96.9 1.3 %spectra.1 = f32[4,2,256,128]{3,2,1,0:T(8,128)} custom-call(f32[1536,128]{1,0:T(8,128)S(1)} %bitcast.6), custom_call_target="tpu_custom_call" | custom-call | tf_op jit(solution)/shard_map/spectra/pallas_call | solution.py:336
Async XLA Ops:
  0.0 32.0 %copy-start = (bf16[8,256,768]{2,1,0:T(8,128)(2,1)S(1)}, bf16[8,256,768]{2,1,0:T(8,128)(2,1)}, u32[]{:S(2)}) copy-start(bf16[8,256,768]{2,1,0:T(8,128)(2,1)} %constant.10.clone.w_ref) | copy-start | bytes 9437188
  0.9 5.5 %collective-permute-start = (s32[6,4,128]{2,1,0:T(4,128)S(1)}, s32[6,4,128]{2,1,0:T(4,128)S(1)}, u32[]{:S(2)}, u32[]{:S(2)}) collective-permute-start(s32[6,4,128]{2,1,0:T(4,128)S(1)} %slice.3), channel_id=1, source_target_pairs={{16,0},{32,16},{48,32},{64,48},{80,64},{96,80},{112,96},{128,112},... | collective-permute-start | bytes 36872 | tf_op jit(solution)/shard_map/ppermute | solution.py:290
  4.1 0.7 copy-start.5
  32.0 44.1 %copy-start.1 = (bf16[768,512]{1,0:T(8,128)(2,1)S(1)}, bf16[768,512]{1,0:T(8,128)(2,1)}, u32[]{:S(2)}) copy-start(bf16[768,512]{1,0:T(8,128)(2,1)} %constant.11.clone.y_ref) | copy-start | bytes 2359300
  32.0 44.1 %copy-start.2 = (bf16[128,768]{1,0:T(8,128)(2,1)S(1)}, bf16[128,768]{1,0:T(8,128)(2,1)}, u32[]{:S(2)}) copy-start(bf16[128,768]{1,0:T(8,128)(2,1)} %constant.14.clone.last_ref) | copy-start | bytes 589828
  32.0 44.1 %copy-start.3 = (f32[128,256]{1,0:T(8,128)S(1)}, f32[128,256]{1,0:T(8,128)}, u32[]{:S(2)}) copy-start(f32[128,256]{1,0:T(8,128)} %constant.13.clone.ti_ref) | copy-start | bytes 393220
  32.0 44.1 %copy-start.4 = (f32[128,256]{1,0:T(8,128)S(1)}, f32[128,256]{1,0:T(8,128)}, u32[]{:S(2)}) copy-start(f32[128,256]{1,0:T(8,128)} %constant.12.clone.tr_ref) | copy-start | bytes 393220

commit v4 on v3

--- a/solution.py
+++ b/solution.py
@@ -12,7 +12,6 @@
 
 VMEM = pl.BlockSpec(memory_space=pltpu.VMEM)
 HBM = pl.BlockSpec(memory_space=pltpu.HBM)
-WIDE = pltpu.CompilerParams(vmem_limit_bytes=54000 * 1024)
 PARAMS = pltpu.CompilerParams(vmem_limit_bytes=48 * 1024 * 1024)
 
 
@@ -44,13 +43,8 @@
 def z_matrices():
     q = np.arange(128)[:, None]
     j = np.arange(128)[None, :]
-
-    def block(s, sign):
-        theta = 2.0 * math.pi / 2048 * ((j * (16 * q + s)) % 2048)
-        return np.concatenate([np.cos(theta), sign * np.sin(theta)], axis=1)
-
-    pairs = [(block(0, 1.0), block(8, 1.0))] + [(block(s, 1.0), block(16 - s, -1.0)) for s in range(1, 8)]
-    return np.stack([joined(np.concatenate(pair, axis=0), 1) for pair in pairs])
+    angles = [2.0 * math.pi / 2048 * ((j * (16 * q + s)) % 2048) for s in range(9)]
+    return np.stack([joined(np.concatenate([np.cos(t), np.sin(t)], axis=1), 1) for t in angles])
 
 
 def y_matrix():
@@ -86,14 +80,14 @@
     return joined(w.reshape(128, 256), 1)
 
 
-def along_x(values, labels):
-    def fill(ids):
-        value = jnp.where(ids == 1, values[1], values[0])
-        for k in range(2, 6):
-            value = jnp.where(ids == k, values[k], value)
-        return value
-
-    f = [fill(ids) for ids in labels]
+def fill(values, ids):
+    value = jnp.where(ids == 1, values[1], values[0])
+    for k in range(2, 6):
+        value = jnp.where(ids == k, values[k], value)
+    return value
+
+
+def along_x(f):
     s = [(f[k] + 6.0 * f[k + 1] + f[k + 2]) * 0.125 for k in range(4)]
     return [s[2] - s[0], s[3] - s[1], s[1], s[2]]
 
@@ -126,7 +120,7 @@
     for b in range(BLOCKS):
         copies[1 + b].wait()
         rows = pl.ds(TALL * b, TALL)
-        for a, value in enumerate(along_x(values, [held[x, rows, :] for x in range(6)])):
+        for a, value in enumerate(along_x([fill(values, held[x, rows, :]) for x in range(6)])):
             ext[a, rows, :] = value
         ready = (TALL * (b + 1) - 3) // 16
         for a in range(4):
@@ -149,7 +143,7 @@
     out_ref[0:15] = in_ref[0:15]
     ext[:, 0:24, :] = end_ref[...]
     values = [table_ref[k : k + 1, :] for k in range(6)]
-    for a, value in enumerate(along_x(values, [next_ref[x] for x in range(6)])):
+    for a, value in enumerate(along_x([fill(values, next_ref[x]) for x in range(6)])):
         ext[a, 24:28, :] = value
         out_ref[15, 16 * a : 16 * a + 16, :] = along_y(ext, a, 8, 16)
     for p in range(2):
@@ -220,17 +214,20 @@
         high, low = split(jnp.concatenate([top, bottom], axis=0))
         return jnp.concatenate([high, high, low], axis=1)
 
-    out_ref[0] = dot_t(w_ref[0, :128, :], arranged(0))
-    out_ref[8] = dot_t(w_ref[0, 128:, :], arranged(8))
-    for k in range(1, 8):
-        both = dot_t(w_ref[k], arranged(k))
-        out_ref[k] = both[:128]
-        out_ref[16 - k] = both[128:] * sign
+    for k in range(9):
+        wave = dot_t(w_ref[k], arranged(k))
+        out_ref[k] = wave
+        if 0 < k < 8:
+            wave = wave * sign
+            for block in range(16):
+                out_ref[16 - k, 8 * block : 8 * block + 8, :] = wave[120 - 8 * block : 128 - 8 * block]
 
 
 def modes_kernel(in_ref, y_ref, tr_ref, ti_ref, last_ref, out_ref):
     tr, ti = tr_ref[...], ti_ref[...]
-    turned = jnp.concatenate([in_ref[pl.ds(q, 256, stride=8), :].T for q in range(8)], axis=0)
+    backwards = lax.axis_index("gy") > 8
+    starts = [jnp.where(backwards, 7 - q, q) for q in range(8)]
+    turned = jnp.concatenate([in_ref[pl.ds(start, 256, stride=8), :].T for start in starts], axis=0)
     high, low = split(turned)
     both = dot(jnp.concatenate([high, high, low], axis=1), y_ref[...])
     for q in range(8):
@@ -299,10 +296,10 @@
             pltpu.VMEM((4, 256, 128), jnp.float32),
             pltpu.SemaphoreType.DMA((BLOCKS + 1,)),
         ],
-        compiler_params=WIDE,
+        compiler_params=PARAMS,
         cost_estimate=pl.CostEstimate(flops=10_000_000, bytes_accessed=4_000_000, transcendentals=0),
         name="planes",
-    )(porosity, labels)
+    )(*[pltpu.with_memory_space_constraint(array, pltpu.HBM) for array in (porosity, labels)])
     rows = pl.pallas_call(
         rows_kernel,
         out_shape=shape(16, 72, 128),

time: 98.4 us -> 97.1 us (0.987)
  blocking collectives: 86.6 us -> 85.6 us
    all_to_all x1, blocking collectives: 42.3 us -> 40.8 us  [shards(): lax.all_to_all(columns.reshape(256, 8, 128), ('gy', 'gz'), 0, 0, tiled=True)]
where the time goes in v4:
time: 97.1 us; the launch traced here: 96.9 us
  blocking collectives  85.6 us (88%)
  Pallas kernels  6.28 us (6%)
  starting transfers between devices  3.24 us (3%)
    all_to_all x1, blocking collectives, shards(): lax.all_to_all(columns.reshape(256, 8, 128), ('gy', 'gz'), 0, 0, tiled=True)  40.8 us
    all_to_all x1, blocking collectives, shards(): rows = lax.all_to_all(rows, 'gz', 0, 0, tiled=True)  26 us
    all_to_all x1, blocking collectives, shards(): modes = lax.all_to_all(modes.reshape(16, 96, 128), 'gy', 0, 0, tiled=True)  18.8 us
    ppermute x1, starting transfers between devices, shards(): lax.ppermute(labels[:, :4, :], 'gy', [((i + 1) % count, i) for i in range...  3.24 us
    pallas_call x1, Pallas kernels, shards(): pl.pallas_call(modes_kernel, out_shape=shape(16 * 96, 128), in_specs=[VME...  2.08 us
  transfers between devices with their start and end apart: 1, of which 1 were waited for; matrix products, arithmetic and copies ran while one was open for 0% of the time, Pallas kernels for 1%

profile of v4, /device:TPU:1, one launch (start us, length us, event | category | flops | bytes accessed | tf_op | source)
XLA Modules:
  0.0 96.9 jit_solution(13139915367720158372)
XLA Ops:
  0.0 0.0 copy-start
  0.0 0.9 slice.3
  0.9 3.2 %collective-permute-start = (s32[6,4,128]{2,1,0:T(4,128)S(1)}, s32[6,4,128]{2,1,0:T(4,128)S(1)}, u32[]{:S(2)}, u32[]{:S(2)}) collective-permute-start(s32[6,4,128]{2,1,0:T(4,128)S(1)} %slice.3), channel_id=1, source_target_pairs={{16,0},{32,16},{48,32},{64,48},{80,64},{96,80},{112,96},{128,112},... | collective-permute-start | bytes 36872 | tf_op jit(solution)/shard_map/ppermute | solution.py:287
  4.1 1.4 %planes.1 = (f32[16,72,128]{2,1,0:T(8,128)S(1)}, f32[4,24,128]{2,1,0:T(8,128)S(1)}, f32[8,128]{1,0:T(8,128)S(1)}) custom-call(f32[6]{0:T(128)} %por_ref.1, s32[6,256,128]{2,1,0:T(8,128)} %lab_ref.1), custom_call_target="tpu_custom_call" | custom-call | flops 10000000 | bytes 4000000 | tf_op jit(solution)/shard_map/planes/pallas_call | solution.py:288
  5.5 0.8 collective-permute-done.next_ref
  6.4 0.1 rows.1
  6.5 26.0 %all_to_all.15.in_ref = f32[16,72,128]{2,1,0:T(8,128)S(1)} all-to-all(f32[16,72,128]{2,1,0:T(8,128)S(1)} %rows.1), channel_id=1, replica_groups=mesh['gy'=16,'gz'=16] {'gz'}, dimensions={0} | all-to-all | bytes 1179648 | tf_op jit(solution)/shard_map/all_to_all | solution.py:312
  32.4 0.0 copy-done
  32.4 1.4 %columns.1 = f32[16,128,128]{2,1,0:T(8,128)S(1)} custom-call(f32[16,72,128]{2,1,0:T(8,128)S(1)} %all_to_all.15.in_ref, bf16[9,128,768]{2,1,0:T(8,128)(2,1)S(1)} %copy-done), custom_call_target="tpu_custom_call" | custom-call | tf_op jit(solution)/shard_map/columns/pallas_call | solution.py:313
  33.8 0.0 copy-start.1
  33.8 0.0 copy-start.2
  33.8 0.0 copy-start.3
  33.8 0.0 copy-start.4
  33.8 40.8 %all_to_all.16 = f32[256,8,128]{2,1,0:T(8,128)S(1)} all-to-all(f32[256,8,128]{2,1,0:T(8,128)S(1)} %bitcast.5), channel_id=1, replica_groups=mesh['gy'=16,'gz'=16] {'gy','gz'}, dimensions={0} | all-to-all | bytes 2097152 | tf_op jit(solution)/shard_map/all_to_all | solution.py:322
  74.7 0.0 copy-done.1
  74.7 0.0 copy-done.2
  74.7 0.0 copy-done.3
  74.7 0.0 copy-done.4
  74.7 2.1 %modes.1 = f32[1536,128]{1,0:T(8,128)S(1)} custom-call(f32[2048,128]{1,0:T(8,128)S(1)} %bitcast.4, bf16[768,512]{1,0:T(8,128)(2,1)S(1)} %copy-done.1, f32[128,256]{1,0:T(8,128)S(1)} %copy-done.4, f32[128,256]{1,0:T(8,128)S(1)} %copy-done.3, bf16[128,768]{1,0:T(8,128)(2,1)S(1)} %copy-done.2), custom_call_target="tpu_custom_call" | custom-call | tf_op jit(solution)/shard_map/modes/pallas_call | solution.py:324
  76.8 18.8 %all_to_all.17 = f32[16,96,128]{2,1,0:T(8,128)S(1)} all-to-all(f32[16,96,128]{2,1,0:T(8,128)S(1)} %bitcast.7), channel_id=1, replica_groups=mesh['gy'=16,'gz'=16] {'gy'}, dimensions={0} | all-to-all | bytes 1572864 | tf_op jit(solution)/shard_map/all_to_all | solution.py:332
  95.6 1.3 %spectra.1 = f32[4,2,256,128]{3,2,1,0:T(8,128)} custom-call(f32[1536,128]{1,0:T(8,128)S(1)} %bitcast.6), custom_call_target="tpu_custom_call" | custom-call | tf_op jit(solution)/shard_map/spectra/pallas_call | solution.py:333
Async XLA Ops:
  0.0 32.4 %copy-start = (bf16[9,128,768]{2,1,0:T(8,128)(2,1)S(1)}, bf16[9,128,768]{2,1,0:T(8,128)(2,1)}, u32[]{:S(2)}) copy-start(bf16[9,128,768]{2,1,0:T(8,128)(2,1)} %constant.10.clone.w_ref) | copy-start | bytes 5308420
  0.9 5.5 %collective-permute-start = (s32[6,4,128]{2,1,0:T(4,128)S(1)}, s32[6,4,128]{2,1,0:T(4,128)S(1)}, u32[]{:S(2)}, u32[]{:S(2)}) collective-permute-start(s32[6,4,128]{2,1,0:T(4,128)S(1)} %slice.3), channel_id=1, source_target_pairs={{16,0},{32,16},{48,32},{64,48},{80,64},{96,80},{112,96},{128,112},... | collective-permute-start | bytes 36872 | tf_op jit(solution)/shard_map/ppermute | solution.py:287
  33.8 40.9 %copy-start.1 = (bf16[768,512]{1,0:T(8,128)(2,1)S(1)}, bf16[768,512]{1,0:T(8,128)(2,1)}, u32[]{:S(2)}) copy-start(bf16[768,512]{1,0:T(8,128)(2,1)} %constant.11.clone.y_ref) | copy-start | bytes 2359300
  33.8 40.9 %copy-start.2 = (bf16[128,768]{1,0:T(8,128)(2,1)S(1)}, bf16[128,768]{1,0:T(8,128)(2,1)}, u32[]{:S(2)}) copy-start(bf16[128,768]{1,0:T(8,128)(2,1)} %constant.14.clone.last_ref) | copy-start | bytes 589828
  33.8 40.9 %copy-start.3 = (f32[128,256]{1,0:T(8,128)S(1)}, f32[128,256]{1,0:T(8,128)}, u32[]{:S(2)}) copy-start(f32[128,256]{1,0:T(8,128)} %constant.13.clone.ti_ref) | copy-start | bytes 393220
  33.8 40.9 %copy-start.4 = (f32[128,256]{1,0:T(8,128)S(1)}, f32[128,256]{1,0:T(8,128)}, u32[]{:S(2)}) copy-start(f32[128,256]{1,0:T(8,128)} %constant.12.clone.tr_ref) | copy-start | bytes 393220

commit v5 on v4

--- a/solution.py
+++ b/solution.py
@@ -100,6 +100,7 @@
     ) * 0.125
 
 
+CHUNK = 68
 BLOCKS = 4
 TALL = 256 // BLOCKS
 
@@ -124,33 +125,36 @@
             ext[a, rows, :] = value
         ready = (TALL * (b + 1) - 3) // 16
         for a in range(4):
-            block = along_y(ext, a, 16 * done, 16 * (ready - done))
-            out_ref[done:ready, 16 * a : 16 * a + 16, :] = block.reshape(ready - done, 16, 128)
+            for d in range(done, ready):
+                at = CHUNK * d + 16 * a
+                out_ref[at : at + 16, :] = along_y(ext, a, 16 * d, 16)
         done = ready
     for p in range(2):
         a = 2 + p
         for d in range(15):
-            below = along_y(ext, a, -1, 1) if d == 0 else out_ref[d - 1, 16 * a + 15 : 16 * a + 16, :]
-            above = along_y(ext, a, 240, 1) if d == 14 else out_ref[d + 1, 16 * a : 16 * a + 1, :]
-            out_ref[d, 64 + 2 * p : 65 + 2 * p, :] = below
-            out_ref[d, 65 + 2 * p : 66 + 2 * p, :] = above
-    out_ref[0:15, 68:72, :] = jnp.zeros((15, 4, 128), jnp.float32)
-    out_ref[15] = jnp.zeros((72, 128), jnp.float32)
+            at = CHUNK * d + 16 * a
+            edge = CHUNK * d + 64 + 2 * p
+            below = along_y(ext, a, -1, 1) if d == 0 else out_ref[at - CHUNK + 15 : at - CHUNK + 16, :]
+            above = along_y(ext, a, 240, 1) if d == 14 else out_ref[at + CHUNK : at + CHUNK + 1, :]
+            out_ref[edge : edge + 1, :] = below
+            out_ref[edge + 1 : edge + 2, :] = above
+    out_ref[15 * CHUNK :, :] = jnp.zeros((CHUNK, 128), jnp.float32)
     end_ref[...] = ext[:, 232:256, :]
 
 
 def rows_kernel(in_ref, end_ref, table_ref, next_ref, out_ref, ext):
-    out_ref[0:15] = in_ref[0:15]
+    last = 15 * CHUNK
+    out_ref[:last, :] = in_ref[:last, :]
     ext[:, 0:24, :] = end_ref[...]
     values = [table_ref[k : k + 1, :] for k in range(6)]
     for a, value in enumerate(along_x([fill(values, next_ref[x]) for x in range(6)])):
         ext[a, 24:28, :] = value
-        out_ref[15, 16 * a : 16 * a + 16, :] = along_y(ext, a, 8, 16)
+        out_ref[last + 16 * a : last + 16 * a + 16, :] = along_y(ext, a, 8, 16)
     for p in range(2):
         a = 2 + p
-        out_ref[15, 64 + 2 * p : 65 + 2 * p, :] = along_y(ext, a, 7, 1)
-        out_ref[15, 65 + 2 * p : 66 + 2 * p, :] = along_y(ext, a, 24, 1)
-    out_ref[15, 68:72, :] = jnp.zeros((4, 128), jnp.float32)
+        edge = last + 64 + 2 * p
+        out_ref[edge : edge + 1, :] = along_y(ext, a, 7, 1)
+        out_ref[edge + 1 : edge + 2, :] = along_y(ext, a, 24, 1)
 
 
 def real_transform(x):
@@ -190,12 +194,15 @@
     def along_z(x):
         return (before(x) + 6.0 * x + after(x)) * 0.125
 
+    def rows(first, count):
+        return jnp.stack([in_ref[CHUNK * d + first : CHUNK * d + first + count, :] for d in range(16)])
+
     for p in range(2):
-        center = in_ref[:, 32 + 16 * p : 48 + 16 * p, :]
+        center = rows(32 + 16 * p, 16)
         ext[:, 8:24, :] = center
-        ext[:, 7:8, :] = in_ref[:, 64 + 2 * p : 65 + 2 * p, :]
-        ext[:, 24:25, :] = in_ref[:, 65 + 2 * p : 66 + 2 * p, :]
-        grad_x = along_z(in_ref[:, 16 * p : 16 * p + 16, :])
+        ext[:, 7:8, :] = rows(64 + 2 * p, 1)
+        ext[:, 24:25, :] = rows(65 + 2 * p, 1)
+        grad_x = along_z(rows(16 * p, 16))
         grad_y = along_z(ext[:, 9:25, :] - ext[:, 7:23, :])
         pore = along_z(center)
         grad_z = after(pore) - before(pore)
@@ -287,7 +294,7 @@
     following = lax.ppermute(labels[:, :4, :], "gy", [((i + 1) % count, i) for i in range(count)])
     planes, ends, table = pl.pallas_call(
         planes_kernel,
-        out_shape=(shape(16, 72, 128), shape(4, 24, 128), shape(8, 128)),
+        out_shape=(shape(16 * CHUNK, 128), shape(4, 24, 128), shape(8, 128)),
         in_specs=[HBM, HBM],
         out_specs=(VMEM, VMEM, VMEM),
         scratch_shapes=[
@@ -302,14 +309,14 @@
     )(*[pltpu.with_memory_space_constraint(array, pltpu.HBM) for array in (porosity, labels)])
     rows = pl.pallas_call(
         rows_kernel,
-        out_shape=shape(16, 72, 128),
+        out_shape=shape(16 * CHUNK, 128),
         in_specs=[VMEM, VMEM, VMEM, VMEM],
         out_specs=VMEM,
         scratch_shapes=[pltpu.VMEM((4, 32, 128), jnp.float32)],
         compiler_params=PARAMS,
         name="rows",
     )(planes, ends, table, following)
-    rows = lax.all_to_all(rows, "gz", 0, 0, tiled=True)
+    rows = lax.all_to_all(rows.reshape(4 * CHUNK, 4, 128), "gz", 0, 0, tiled=True).reshape(16 * CHUNK, 128)
     columns = pl.pallas_call(
         columns_kernel,
         out_shape=shape(16, 128, 128),

time: 97.1 us -> 96.4 us (level)
  no operation moved by 1% of the time
where the time goes in v5:
time: 96.4 us; the launch traced here: 96.2 us
  blocking collectives  84.9 us (88%)
  Pallas kernels  6.28 us (7%)
  starting transfers between devices  3.24 us (3%)
    all_to_all x1, blocking collectives, shards(): lax.all_to_all(columns.reshape(256, 8, 128), ('gy', 'gz'), 0, 0, tiled=True)  40.6 us
    all_to_all x1, blocking collectives, shards(): lax.all_to_all(rows.reshape(4 * CHUNK, 4, 128), 'gz', 0, 0, tiled=True)  25.6 us
    all_to_all x1, blocking collectives, shards(): modes = lax.all_to_all(modes.reshape(16, 96, 128), 'gy', 0, 0, tiled=True)  18.8 us
    ppermute x1, starting transfers between devices, shards(): lax.ppermute(labels[:, :4, :], 'gy', [((i + 1) % count, i) for i in range...  3.24 us
    pallas_call x1, Pallas kernels, shards(): pl.pallas_call(modes_kernel, out_shape=shape(16 * 96, 128), in_specs=[VME...  2.08 us
  transfers between devices with their start and end apart: 1, of which 1 were waited for; matrix products, arithmetic and copies ran while one was open for 0% of the time, Pallas kernels for 1%

profile of v5, /device:TPU:1, one launch (start us, length us, event | category | flops | bytes accessed | tf_op | source)
XLA Modules:
  0.0 96.2 jit_solution(6147785768796196047)
XLA Ops:
  0.0 0.0 copy-start
  0.0 0.9 slice.3
  0.9 3.2 %collective-permute-start = (s32[6,4,128]{2,1,0:T(4,128)S(1)}, s32[6,4,128]{2,1,0:T(4,128)S(1)}, u32[]{:S(2)}, u32[]{:S(2)}) collective-permute-start(s32[6,4,128]{2,1,0:T(4,128)S(1)} %slice.3), channel_id=1, source_target_pairs={{16,0},{32,16},{48,32},{64,48},{80,64},{96,80},{112,96},{128,112},... | collective-permute-start | bytes 36872 | tf_op jit(solution)/shard_map/ppermute | solution.py:294
  4.1 1.4 %planes.1 = (f32[1088,128]{1,0:T(8,128)S(1)}, f32[4,24,128]{2,1,0:T(8,128)S(1)}, f32[8,128]{1,0:T(8,128)S(1)}) custom-call(f32[6]{0:T(128)} %por_ref.1, s32[6,256,128]{2,1,0:T(8,128)} %lab_ref.1), custom_call_target="tpu_custom_call" | custom-call | flops 10000000 | bytes 4000000 | tf_op jit(solution)/shard_map/planes/pallas_call | solution.py:295
  5.5 0.8 collective-permute-done.next_ref
  6.4 0.1 rows.1
  6.5 25.6 %all_to_all.15 = f32[272,4,128]{2,1,0:T(4,128)S(1)} all-to-all(f32[272,4,128]{2,1,0:T(4,128)S(1)} %bitcast.11), channel_id=1, replica_groups=mesh['gy'=16,'gz'=16] {'gz'}, dimensions={0} | all-to-all | bytes 1114112 | tf_op jit(solution)/shard_map/all_to_all | solution.py:319
  32.0 0.0 copy-done
  32.0 1.4 %columns.1 = f32[16,128,128]{2,1,0:T(8,128)S(1)} custom-call(f32[1088,128]{1,0:T(8,128)S(1)} %bitcast.10, bf16[9,128,768]{2,1,0:T(8,128)(2,1)S(1)} %copy-done), custom_call_target="tpu_custom_call" | custom-call | tf_op jit(solution)/shard_map/columns/pallas_call | solution.py:320
  33.4 0.0 copy-start.1
  33.4 0.0 copy-start.2
  33.4 0.0 copy-start.3
  33.4 0.0 copy-start.4
  33.4 40.6 %all_to_all.16 = f32[256,8,128]{2,1,0:T(8,128)S(1)} all-to-all(f32[256,8,128]{2,1,0:T(8,128)S(1)} %bitcast.7), channel_id=1, replica_groups=mesh['gy'=16,'gz'=16] {'gy','gz'}, dimensions={0} | all-to-all | bytes 2097152 | tf_op jit(solution)/shard_map/all_to_all | solution.py:329
  74.0 0.0 copy-done.1
  74.0 0.0 copy-done.2
  74.0 0.0 copy-done.3
  74.0 0.0 copy-done.4
  74.0 2.1 %modes.1 = f32[1536,128]{1,0:T(8,128)S(1)} custom-call(f32[2048,128]{1,0:T(8,128)S(1)} %bitcast.6, bf16[768,512]{1,0:T(8,128)(2,1)S(1)} %copy-done.1, f32[128,256]{1,0:T(8,128)S(1)} %copy-done.4, f32[128,256]{1,0:T(8,128)S(1)} %copy-done.3, bf16[128,768]{1,0:T(8,128)(2,1)S(1)} %copy-done.2), custom_call_target="tpu_custom_call" | custom-call | tf_op jit(solution)/shard_map/modes/pallas_call | solution.py:331
  76.1 18.8 %all_to_all.17 = f32[16,96,128]{2,1,0:T(8,128)S(1)} all-to-all(f32[16,96,128]{2,1,0:T(8,128)S(1)} %bitcast.9), channel_id=1, replica_groups=mesh['gy'=16,'gz'=16] {'gy'}, dimensions={0} | all-to-all | bytes 1572864 | tf_op jit(solution)/shard_map/all_to_all | solution.py:339
  94.9 1.3 %spectra.1 = f32[4,2,256,128]{3,2,1,0:T(8,128)} custom-call(f32[1536,128]{1,0:T(8,128)S(1)} %bitcast.8), custom_call_target="tpu_custom_call" | custom-call | tf_op jit(solution)/shard_map/spectra/pallas_call | solution.py:340
Async XLA Ops:
  0.0 32.0 %copy-start = (bf16[9,128,768]{2,1,0:T(8,128)(2,1)S(1)}, bf16[9,128,768]{2,1,0:T(8,128)(2,1)}, u32[]{:S(2)}) copy-start(bf16[9,128,768]{2,1,0:T(8,128)(2,1)} %constant.10.clone.w_ref) | copy-start | bytes 5308420
  0.9 5.5 %collective-permute-start = (s32[6,4,128]{2,1,0:T(4,128)S(1)}, s32[6,4,128]{2,1,0:T(4,128)S(1)}, u32[]{:S(2)}, u32[]{:S(2)}) collective-permute-start(s32[6,4,128]{2,1,0:T(4,128)S(1)} %slice.3), channel_id=1, source_target_pairs={{16,0},{32,16},{48,32},{64,48},{80,64},{96,80},{112,96},{128,112},... | collective-permute-start | bytes 36872 | tf_op jit(solution)/shard_map/ppermute | solution.py:294
  33.4 40.6 %copy-start.1 = (bf16[768,512]{1,0:T(8,128)(2,1)S(1)}, bf16[768,512]{1,0:T(8,128)(2,1)}, u32[]{:S(2)}) copy-start(bf16[768,512]{1,0:T(8,128)(2,1)} %constant.11.clone.y_ref) | copy-start | bytes 2359300
  33.4 40.6 %copy-start.2 = (bf16[128,768]{1,0:T(8,128)(2,1)S(1)}, bf16[128,768]{1,0:T(8,128)(2,1)}, u32[]{:S(2)}) copy-start(bf16[128,768]{1,0:T(8,128)(2,1)} %constant.14.clone.last_ref) | copy-start | bytes 589828
  33.4 40.6 %copy-start.3 = (f32[128,256]{1,0:T(8,128)S(1)}, f32[128,256]{1,0:T(8,128)}, u32[]{:S(2)}) copy-start(f32[128,256]{1,0:T(8,128)} %constant.13.clone.ti_ref) | copy-start | bytes 393220
  33.4 40.6 %copy-start.4 = (f32[128,256]{1,0:T(8,128)S(1)}, f32[128,256]{1,0:T(8,128)}, u32[]{:S(2)}) copy-start(f32[128,256]{1,0:T(8,128)} %constant.12.clone.tr_ref) | copy-start | bytes 393220

commit v6 on v5

--- a/solution.py
+++ b/solution.py
@@ -40,11 +40,36 @@
     return np.concatenate([high, low, high], axis=axis)
 
 
+PAIRED = (1, 2, 3, 5, 6, 7, 9, 10, 11, 13, 14, 15)
+SINGLE = (0, 4, 8, 12)
+DOUBLES = (1, 2, 3, 5, 6, 7)
+
+
 def z_matrices():
-    q = np.arange(128)[:, None]
     j = np.arange(128)[None, :]
-    angles = [2.0 * math.pi / 2048 * ((j * (16 * q + s)) % 2048) for s in range(9)]
-    return np.stack([joined(np.concatenate([np.cos(t), np.sin(t)], axis=1), 1) for t in angles])
+
+    def block(s, count):
+        theta = 2.0 * math.pi / 2048 * ((j * (16 * np.arange(count)[:, None] + s)) % 2048)
+        return np.concatenate([np.cos(theta), np.sin(theta) * (1.0 if s <= 8 else -1.0)], axis=1)
+
+    blocks = [block(s, 128) for s in (0, 8, 4, 12)]
+    for k in DOUBLES:
+        blocks += [block(k, 64), block(16 - k, 64)]
+    return joined(np.concatenate(blocks, axis=0), 1)
+
+
+def order_matrices():
+    out = np.zeros((2, 4, 32, 128))
+    for source in range(32):
+        side, (i, b) = source // 16, divmod(source % 16, 2)
+        combo = 2 * b + side
+        for slot in range(3):
+            t = 16 * i + PAIRED[3 * combo + slot]
+            out[0, slot, source, t] = 1.0
+            out[1, slot, source, 128 - t] = 1.0
+        out[:, 3, source, 16 * i + SINGLE[combo]] = 1.0
+    out = out.reshape(2, 128, 128)
+    return np.concatenate([out, out], axis=1).astype(ml_dtypes.bfloat16)
 
 
 def y_matrix():
@@ -77,7 +102,9 @@
             w[2 * field + 1, plane, :, 1, 0, field, plane] = -cos
             w[2 * field + 1, plane, :, 0, 0, field, plane] = -sin
             w[2 * field + 1, plane, :, 1, 1, field, plane] = -sin
-    return joined(w.reshape(128, 256), 1)
+    mirrored = w.copy()
+    mirrored[:, :, :, :, 1] *= -1.0
+    return joined(np.concatenate([w.reshape(128, 256), mirrored.reshape(128, 256)], axis=0), 1)
 
 
 def fill(values, ids):
@@ -221,26 +248,34 @@
         high, low = split(jnp.concatenate([top, bottom], axis=0))
         return jnp.concatenate([high, high, low], axis=1)
 
-    for k in range(9):
-        wave = dot_t(w_ref[k], arranged(k))
-        out_ref[k] = wave
-        if 0 < k < 8:
-            wave = wave * sign
-            for block in range(16):
-                out_ref[16 - k, 8 * block : 8 * block + 8, :] = wave[120 - 8 * block : 128 - 8 * block]
+    def send(wave, s, blocks):
+        paired = s in PAIRED
+        combo, slot = divmod(PAIRED.index(s), 3) if paired else (SINGLE.index(s), 3)
+        b, side = divmod(combo, 2)
+        for block in range(blocks):
+            low = min(block, 15 - block)
+            gz = 15 - low if side else low
+            at = 5 * (16 * b + gz) + slot + (1 if block > 7 else 0)
+            out_ref[pl.ds(at, 8, stride=160), :] = wave[8 * block : 8 * block + 8]
+
+    send(dot_t(w_ref[0:128, :], arranged(0)), 0, 16)
+    send(dot_t(w_ref[128:256, :], arranged(8)), 8, 16)
+    both = dot_t(w_ref[256:512, :], arranged(4))
+    send(both[:128], 4, 16)
+    send(both[128:] * sign, 12, 16)
+    for e, k in enumerate(DOUBLES):
+        both = dot_t(w_ref[512 + 128 * e : 640 + 128 * e, :], arranged(k))
+        send(both[:64], k, 8)
+        send(both[64:] * sign[:64], 16 - k, 8)
 
 
 def modes_kernel(in_ref, y_ref, tr_ref, ti_ref, last_ref, out_ref):
     tr, ti = tr_ref[...], ti_ref[...]
-    backwards = lax.axis_index("gy") > 8
-    starts = [jnp.where(backwards, 7 - q, q) for q in range(8)]
-    turned = jnp.concatenate([in_ref[pl.ds(start, 256, stride=8), :].T for start in starts], axis=0)
+    turned = jnp.concatenate([in_ref[pl.ds(slot, 256, stride=5), :].T for slot in range(5)], axis=0)
     high, low = split(turned)
     both = dot(jnp.concatenate([high, high, low], axis=1), y_ref[...])
-    for q in range(8):
-        cos, sin = both[128 * q : 128 * q + 128, :256], both[128 * q : 128 * q + 128, 256:]
-        high, low = split(jnp.concatenate([cos * tr + sin * ti, sin * tr - cos * ti], axis=0))
-        modes = dot(last_ref[...], jnp.concatenate([high, high, low], axis=0))
+
+    def write(modes, side, column):
         sr, si, pr, pi = modes[:32], modes[32:64], modes[64:96], modes[96:]
         square = sr * sr + si * si
         some = square > 1e-30
@@ -254,27 +289,44 @@
             for p in range(2):
                 for half in range(2):
                     block = result[16 * p : 16 * p + 16, 128 * half : 128 * half + 128]
-                    out_ref[pl.ds(place(o, p, half, q), 16, stride=96), :] = block
-
-
-def place(o, p, half, q):
-    return 32 * o + 16 * p + 8 * half + q
-
-
-def spectra_kernel(in_ref, out_ref, held, sems):
+                    out_ref[pl.ds(16 * 48 * side + place(o, p, half, column), 16, stride=48), :] = block
+
+    for slot in range(5):
+        cos, sin = both[128 * slot : 128 * slot + 128, :256], both[128 * slot : 128 * slot + 128, 256:]
+        high, low = split(jnp.concatenate([cos * tr + sin * ti, sin * tr - cos * ti], axis=0))
+        data = jnp.concatenate([high, high, low], axis=0)
+        if slot < 3:
+            modes = dot(last_ref[...], data)
+            write(modes[:128], 0, slot)
+            write(modes[128:], 1, slot)
+        else:
+            write(dot(last_ref[:128, :], data), slot - 3, 3)
+
+
+def place(o, p, half, column):
+    return 16 * o + 8 * p + 4 * half + column
+
+
+def spectra_kernel(in_ref, order_ref, out_ref, held, sems):
     factor = 64.0 / (4096 * 2048)
     row = lax.broadcasted_iota(jnp.int32, (128, 128), 0)
     col = lax.broadcasted_iota(jnp.int32, (128, 128), 1)
-    device = lax.axis_index("gy") + lax.axis_index("gz")
-    drop = row + col + device == 0
+    gz = lax.axis_index("gz")
+    drop = row + col + lax.axis_index("gy") + gz == 0
+    order = order_ref[jnp.where(gz > 7, 1, 0)]
     copies = []
     for p in range(2):
         for half in range(2):
             at = 2 * p + half
-            size, re, im = [
-                jnp.concatenate([in_ref[pl.ds(place(o, p, half, q), 16, stride=96), :] for q in range(8)], axis=0).T
+            turned = [
+                jnp.concatenate(
+                    [in_ref[pl.ds(place(o, p, half, column), 32, stride=48), :] for column in range(4)], axis=0
+                ).T
                 for o in range(3)
             ]
+            high, low = split(jnp.concatenate(turned, axis=0))
+            sorted_values = dot(jnp.concatenate([high, low], axis=1), order)
+            size, re, im = sorted_values[:128], sorted_values[128:256], sorted_values[256:]
             scaled = size * factor
             results = (size * scaled, (re * re + im * im) * factor, scaled * re, scaled * im)
             for o, result in enumerate(results):
@@ -319,33 +371,34 @@
     rows = lax.all_to_all(rows.reshape(4 * CHUNK, 4, 128), "gz", 0, 0, tiled=True).reshape(16 * CHUNK, 128)
     columns = pl.pallas_call(
         columns_kernel,
-        out_shape=shape(16, 128, 128),
+        out_shape=shape(256 * 5, 128),
         in_specs=[VMEM, VMEM],
         out_specs=VMEM,
         scratch_shapes=[pltpu.VMEM((16, 32, 128), jnp.float32), pltpu.VMEM((16, 64, 128), jnp.float32)],
         compiler_params=PARAMS,
         name="columns",
     )(rows, jnp.asarray(z_matrices()))
-    columns = lax.all_to_all(columns.reshape(256, 8, 128), ("gy", "gz"), 0, 0, tiled=True)
+    columns = lax.all_to_all(columns.reshape(256 * 5, 1, 128), ("gy", "gz"), 0, 0, tiled=True)
     cos, sin = twiddles()
     modes = pl.pallas_call(
         modes_kernel,
-        out_shape=shape(16 * 96, 128),
+        out_shape=shape(32 * 48, 128),
         in_specs=[VMEM] * 5,
         out_specs=VMEM,
         compiler_params=PARAMS,
         name="modes",
-    )(columns.reshape(2048, 128), jnp.asarray(y_matrix()), jnp.asarray(cos), jnp.asarray(sin), jnp.asarray(last_matrix()))
-    modes = lax.all_to_all(modes.reshape(16, 96, 128), "gy", 0, 0, tiled=True)
+    )(columns.reshape(256 * 5, 128), jnp.asarray(y_matrix()), jnp.asarray(cos), jnp.asarray(sin), jnp.asarray(last_matrix()))
+    groups = [[16 * gy + gz for gz in (g, 15 - g) for gy in range(16)] for g in range(8)]
+    modes = lax.all_to_all(modes.reshape(32, 48, 128), ("gy", "gz"), 0, 0, tiled=True, axis_index_groups=groups)
     return pl.pallas_call(
         spectra_kernel,
         out_shape=shape(4, 2, 256, 128),
-        in_specs=[VMEM],
+        in_specs=[VMEM, VMEM],
         out_specs=HBM,
         scratch_shapes=[pltpu.VMEM((4, 4, 128, 128), jnp.float32), pltpu.SemaphoreType.DMA((4,))],
         compiler_params=PARAMS,
         name="spectra",
-    )(modes.reshape(16 * 96, 128))
+    )(modes.reshape(32 * 48, 128), jnp.asarray(order_matrices()))
 
 
 def solution(mesh):

time: 96.4 us -> 97.9 us (1.016)
  blocking collectives: 84.9 us -> 86.9 us
    all_to_all x2, blocking collectives: 59.3 us -> 61.3 us  [the longest x1 32.7 us: shards(): lax.all_to_all(columns.reshape(256 * 5, 1, 128), ('gy', 'gz'), 0, 0, tile...]
where the time goes in v6:
time: 97.9 us; the launch traced here: 97.7 us
  blocking collectives  86.9 us (89%)
  Pallas kernels  5.74 us (6%)
  starting transfers between devices  3.24 us (3%)
    all_to_all x1, blocking collectives, shards(): lax.all_to_all(columns.reshape(256 * 5, 1, 128), ('gy', 'gz'), 0, 0, tile...  32.7 us
    all_to_all x1, blocking collectives, shards(): lax.all_to_all(modes.reshape(32, 48, 128), ('gy', 'gz'), 0, 0, tiled=True...  28.6 us
    all_to_all x1, blocking collectives, shards(): lax.all_to_all(rows.reshape(4 * CHUNK, 4, 128), 'gz', 0, 0, tiled=True)  25.6 us
    ppermute x1, starting transfers between devices, shards(): lax.ppermute(labels[:, :4, :], 'gy', [((i + 1) % count, i) for i in range...  3.24 us
  transfers between devices with their start and end apart: 1, of which 1 were waited for; matrix products, arithmetic and copies ran while one was open for 0% of the time, Pallas kernels for 1%

profile of v6, /device:TPU:1, one launch (start us, length us, event | category | flops | bytes accessed | tf_op | source)
XLA Modules:
  0.0 97.7 jit_solution(10953514295908800161)
XLA Ops:
  0.0 0.0 copy-start
  0.0 0.9 slice.3
  0.9 3.2 %collective-permute-start = (s32[6,4,128]{2,1,0:T(4,128)S(1)}, s32[6,4,128]{2,1,0:T(4,128)S(1)}, u32[]{:S(2)}, u32[]{:S(2)}) collective-permute-start(s32[6,4,128]{2,1,0:T(4,128)S(1)} %slice.3), channel_id=1, source_target_pairs={{16,0},{32,16},{48,32},{64,48},{80,64},{96,80},{112,96},{128,112},... | collective-permute-start | bytes 36872 | tf_op jit(solution)/shard_map/ppermute | solution.py:346
  4.1 1.4 %planes.1 = (f32[1088,128]{1,0:T(8,128)S(1)}, f32[4,24,128]{2,1,0:T(8,128)S(1)}, f32[8,128]{1,0:T(8,128)S(1)}) custom-call(f32[6]{0:T(128)} %por_ref.1, s32[6,256,128]{2,1,0:T(8,128)} %lab_ref.1), custom_call_target="tpu_custom_call" | custom-call | flops 10000000 | bytes 4000000 | tf_op jit(solution)/shard_map/planes/pallas_call | solution.py:347
  5.6 0.8 collective-permute-done.next_ref
  6.4 0.1 rows.1
  6.5 25.6 %all_to_all.15 = f32[272,4,128]{2,1,0:T(4,128)S(1)} all-to-all(f32[272,4,128]{2,1,0:T(4,128)S(1)} %bitcast.12), channel_id=1, replica_groups=mesh['gy'=16,'gz'=16] {'gz'}, dimensions={0} | all-to-all | bytes 1114112 | tf_op jit(solution)/shard_map/all_to_all | solution.py:371
  32.0 0.0 copy-done
  32.0 0.0 copy-start.1
  32.0 0.0 copy-start.2
  32.0 0.0 copy-start.3
  32.0 0.0 copy-start.4
  32.0 1.6 %columns.1 = f32[1280,128]{1,0:T(8,128)S(1)} custom-call(f32[1088,128]{1,0:T(8,128)S(1)} %bitcast.13, bf16[1280,768]{1,0:T(8,128)(2,1)S(1)} %copy-done), custom_call_target="tpu_custom_call" | custom-call | tf_op jit(solution)/shard_map/columns/pallas_call | solution.py:372
  33.6 32.7 %all_to_all.16 = f32[1280,1,128]{2,1,0:T(1,128)S(1)} all-to-all(f32[1280,1,128]{2,1,0:T(1,128)S(1)} %bitcast.11), channel_id=1, replica_groups=mesh['gy'=16,'gz'=16] {'gy','gz'}, dimensions={0} | all-to-all | bytes 1310720 | tf_op jit(solution)/shard_map/all_to_all | solution.py:381
  66.3 0.0 copy-done.1
  66.3 0.0 copy-done.2
  66.3 0.0 copy-done.3
  66.3 0.0 copy-done.4
  66.3 0.0 copy-start.5
  66.4 1.3 %modes.1 = f32[1536,128]{1,0:T(8,128)S(1)} custom-call(f32[1280,128]{1,0:T(8,128)S(1)} %bitcast.10, bf16[768,512]{1,0:T(8,128)(2,1)S(1)} %copy-done.1, f32[128,256]{1,0:T(8,128)S(1)} %copy-done.4, f32[128,256]{1,0:T(8,128)S(1)} %copy-done.3, bf16[256,768]{1,0:T(8,128)(2,1)S(1)} %copy-done.2), custom_call_target="tpu_custom_call" | custom-call | tf_op jit(solution)/shard_map/modes/pallas_call | solution.py:383
  67.7 28.6 %all_to_all.17 = f32[32,48,128]{2,1,0:T(8,128)S(1)} all-to-all(f32[32,48,128]{2,1,0:T(8,128)S(1)} %bitcast.8), channel_id=1, replica_groups={{0,16,32,48,64,80,96,112,128,144,160,176,192,208,224,240,15,31,47,63,79..., dimensions={0} | all-to-all | bytes 1572864 | tf_op jit(solution)/shard_map/all_to_all | solution.py:392
  96.3 0.0 copy-done.5
  96.3 1.3 %spectra.1 = f32[4,2,256,128]{3,2,1,0:T(8,128)} custom-call(f32[1536,128]{1,0:T(8,128)S(1)} %bitcast.9, bf16[2,256,128]{2,1,0:T(8,128)(2,1)S(1)} %copy-done.5), custom_call_target="tpu_custom_call" | custom-call | tf_op jit(solution)/shard_map/spectra/pallas_call | solution.py:393
Async XLA Ops:
  0.0 32.0 %copy-start = (bf16[1280,768]{1,0:T(8,128)(2,1)S(1)}, bf16[1280,768]{1,0:T(8,128)(2,1)}, u32[]{:S(2)}) copy-start(bf16[1280,768]{1,0:T(8,128)(2,1)} %constant.12.clone.w_ref) | copy-start | bytes 5898244
  0.9 5.5 %collective-permute-start = (s32[6,4,128]{2,1,0:T(4,128)S(1)}, s32[6,4,128]{2,1,0:T(4,128)S(1)}, u32[]{:S(2)}, u32[]{:S(2)}) collective-permute-start(s32[6,4,128]{2,1,0:T(4,128)S(1)} %slice.3), channel_id=1, source_target_pairs={{16,0},{32,16},{48,32},{64,48},{80,64},{96,80},{112,96},{128,112},... | collective-permute-start | bytes 36872 | tf_op jit(solution)/shard_map/ppermute | solution.py:346
  32.0 34.3 %copy-start.1 = (bf16[768,512]{1,0:T(8,128)(2,1)S(1)}, bf16[768,512]{1,0:T(8,128)(2,1)}, u32[]{:S(2)}) copy-start(bf16[768,512]{1,0:T(8,128)(2,1)} %constant.13.clone.y_ref) | copy-start | bytes 2359300
  32.0 34.3 %copy-start.2 = (bf16[256,768]{1,0:T(8,128)(2,1)S(1)}, bf16[256,768]{1,0:T(8,128)(2,1)}, u32[]{:S(2)}) copy-start(bf16[256,768]{1,0:T(8,128)(2,1)} %constant.16.clone.last_ref) | copy-start | bytes 1179652
  32.0 34.3 %copy-start.3 = (f32[128,256]{1,0:T(8,128)S(1)}, f32[128,256]{1,0:T(8,128)}, u32[]{:S(2)}) copy-start(f32[128,256]{1,0:T(8,128)} %constant.15.clone.ti_ref) | copy-start | bytes 393220
  32.0 34.3 %copy-start.4 = (f32[128,256]{1,0:T(8,128)S(1)}, f32[128,256]{1,0:T(8,128)}, u32[]{:S(2)}) copy-start(f32[128,256]{1,0:T(8,128)} %constant.14.clone.tr_ref) | copy-start | bytes 393220
  66.3 30.0 %copy-start.5 = (bf16[2,256,128]{2,1,0:T(8,128)(2,1)S(1)}, bf16[2,256,128]{2,1,0:T(8,128)(2,1)}, u32[]{:S(2)}) copy-start(bf16[2,256,128]{2,1,0:T(8,128)(2,1)} %constant.17.clone.order_ref) | copy-start | bytes 393220

commit v7 on v5

--- a/solution.py
+++ b/solution.py
@@ -48,15 +48,18 @@
 
 
 def y_matrix():
-    i = np.arange(256)[:, None]
-    m = np.arange(256)[None, :]
-    theta = 2.0 * math.pi / 256 * ((i * m) % 256)
-    return joined(np.concatenate([np.cos(theta), np.sin(theta)], axis=1), 0)
+    i = np.arange(128)[:, None]
+    blocks = []
+    for odd in range(2):
+        m = 2 * np.arange(128)[None, :] + odd
+        theta = 2.0 * math.pi / 256 * ((i * m) % 256)
+        blocks.append(joined(np.concatenate([np.cos(theta), np.sin(theta)], axis=1), 0))
+    return np.concatenate(blocks, axis=0)
 
 
 def twiddles():
     r = np.arange(128)[:, None] % 16
-    m = np.arange(256)[None, :]
+    m = np.concatenate([np.arange(0, 256, 2), np.arange(1, 256, 2)])[None, :]
     phi = 2.0 * math.pi / 4096 * (m * r)
     return np.cos(phi).astype(np.float32), (-np.sin(phi)).astype(np.float32)
 
@@ -232,13 +235,16 @@
 
 def modes_kernel(in_ref, y_ref, tr_ref, ti_ref, last_ref, out_ref):
     tr, ti = tr_ref[...], ti_ref[...]
-    backwards = lax.axis_index("gy") > 8
-    starts = [jnp.where(backwards, 7 - q, q) for q in range(8)]
-    turned = jnp.concatenate([in_ref[pl.ds(start, 256, stride=8), :].T for start in starts], axis=0)
-    high, low = split(turned)
-    both = dot(jnp.concatenate([high, high, low], axis=1), y_ref[...])
+    turned = jnp.concatenate([in_ref[pl.ds(q, 256, stride=8), :].T for q in range(8)], axis=0)
+    halves_of_modes = []
+    for odd in range(2):
+        high, low = split(turned[:, :128] - turned[:, 128:] if odd else turned[:, :128] + turned[:, 128:])
+        part = dot(jnp.concatenate([high, high, low], axis=1), y_ref[384 * odd : 384 * odd + 384, :])
+        halves_of_modes.append(part)
     for q in range(8):
-        cos, sin = both[128 * q : 128 * q + 128, :256], both[128 * q : 128 * q + 128, 256:]
+        parts = [part[128 * q : 128 * q + 128] for part in halves_of_modes]
+        cos = jnp.concatenate([part[:, :128] for part in parts], axis=1)
+        sin = jnp.concatenate([part[:, 128:] for part in parts], axis=1)
         high, low = split(jnp.concatenate([cos * tr + sin * ti, sin * tr - cos * ti], axis=0))
         modes = dot(last_ref[...], jnp.concatenate([high, high, low], axis=0))
         sr, si, pr, pi = modes[:32], modes[32:64], modes[64:96], modes[96:]
@@ -267,20 +273,26 @@
     col = lax.broadcasted_iota(jnp.int32, (128, 128), 1)
     device = lax.axis_index("gy") + lax.axis_index("gz")
     drop = row + col + device == 0
+    eighth = lax.broadcasted_iota(jnp.int32, (8, 128), 0) == 0
+
+    def received(o, p, odd):
+        blocks = [in_ref[pl.ds(place(o, p, odd, q), 16, stride=96), :] for q in range(8)]
+        upper = [jnp.where(eighth, blocks[q][8:], blocks[7 - q][8:]) for q in range(8)]
+        return jnp.concatenate([half for q in range(8) for half in (blocks[q][:8], upper[q])], axis=0)
+
     copies = []
     for p in range(2):
-        for half in range(2):
-            at = 2 * p + half
-            size, re, im = [
-                jnp.concatenate([in_ref[pl.ds(place(o, p, half, q), 16, stride=96), :] for q in range(8)], axis=0).T
-                for o in range(3)
-            ]
+        for odd in range(2):
+            size, re, im = [received(o, p, odd).T for o in range(3)]
             scaled = size * factor
             results = (size * scaled, (re * re + im * im) * factor, scaled * re, scaled * im)
             for o, result in enumerate(results):
-                held[at, o] = jnp.where(drop, 0.0, result) if half == 0 else result
-            copies.append(pltpu.make_async_copy(held.at[at], out_ref.at[:, p, pl.ds(128 * half, 128), :], sems.at[at]))
-            copies[-1].start()
+                result = result if odd else jnp.where(drop, 0.0, result)
+                held[pl.ds(256 * (4 * p + o) + odd, 128, stride=2), :] = result
+                if odd:
+                    source = held.at[pl.ds(256 * (4 * p + o), 256), :]
+                    copies.append(pltpu.make_async_copy(source, out_ref.at[o, p], sems.at[4 * p + o]))
+                    copies[-1].start()
     for copy in copies:
         copy.wait()
 
@@ -342,7 +354,7 @@
         out_shape=shape(4, 2, 256, 128),
         in_specs=[VMEM],
         out_specs=HBM,
-        scratch_shapes=[pltpu.VMEM((4, 4, 128, 128), jnp.float32), pltpu.SemaphoreType.DMA((4,))],
+        scratch_shapes=[pltpu.VMEM((8 * 256, 128), jnp.float32), pltpu.SemaphoreType.DMA((8,))],
         compiler_params=PARAMS,
         name="spectra",
     )(modes.reshape(16 * 96, 128))

time: 96.4 us -> 96.2 us (level)
  no operation moved by 1% of the time
where the time goes in v7:
time: 96.2 us; the launch traced here: 96 us
  blocking collectives  84.9 us (88%)
  Pallas kernels  6.01 us (6%)
  starting transfers between devices  3.24 us (3%)
    all_to_all x1, blocking collectives, shards(): lax.all_to_all(columns.reshape(256, 8, 128), ('gy', 'gz'), 0, 0, tiled=True)  40.6 us
    all_to_all x1, blocking collectives, shards(): lax.all_to_all(rows.reshape(4 * CHUNK, 4, 128), 'gz', 0, 0, tiled=True)  25.6 us
    all_to_all x1, blocking collectives, shards(): modes = lax.all_to_all(modes.reshape(16, 96, 128), 'gy', 0, 0, tiled=True)  18.8 us
    ppermute x1, starting transfers between devices, shards(): lax.ppermute(labels[:, :4, :], 'gy', [((i + 1) % count, i) for i in range...  3.24 us
  transfers between devices with their start and end apart: 1, of which 1 were waited for; matrix products, arithmetic and copies ran while one was open for 0% of the time, Pallas kernels for 1%

profile of v7, /device:TPU:1, one launch (start us, length us, event | category | flops | bytes accessed | tf_op | source)
XLA Modules:
  0.0 96.0 jit_solution(4980163772160723922)
XLA Ops:
  0.0 0.0 copy-start
  0.0 0.9 slice.3
  0.9 3.2 %collective-permute-start = (s32[6,4,128]{2,1,0:T(4,128)S(1)}, s32[6,4,128]{2,1,0:T(4,128)S(1)}, u32[]{:S(2)}, u32[]{:S(2)}) collective-permute-start(s32[6,4,128]{2,1,0:T(4,128)S(1)} %slice.3), channel_id=1, source_target_pairs={{16,0},{32,16},{48,32},{64,48},{80,64},{96,80},{112,96},{128,112},... | collective-permute-start | bytes 36872 | tf_op jit(solution)/shard_map/ppermute | solution.py:306
  4.1 1.4 %planes.1 = (f32[1088,128]{1,0:T(8,128)S(1)}, f32[4,24,128]{2,1,0:T(8,128)S(1)}, f32[8,128]{1,0:T(8,128)S(1)}) custom-call(f32[6]{0:T(128)} %por_ref.1, s32[6,256,128]{2,1,0:T(8,128)} %lab_ref.1), custom_call_target="tpu_custom_call" | custom-call | flops 10000000 | bytes 4000000 | tf_op jit(solution)/shard_map/planes/pallas_call | solution.py:307
  5.5 0.8 collective-permute-done.next_ref
  6.4 0.1 rows.1
  6.5 25.6 %all_to_all.15 = f32[272,4,128]{2,1,0:T(4,128)S(1)} all-to-all(f32[272,4,128]{2,1,0:T(4,128)S(1)} %bitcast.11), channel_id=1, replica_groups=mesh['gy'=16,'gz'=16] {'gz'}, dimensions={0} | all-to-all | bytes 1114112 | tf_op jit(solution)/shard_map/all_to_all | solution.py:331
  32.0 0.0 copy-done
  32.0 1.4 %columns.1 = f32[16,128,128]{2,1,0:T(8,128)S(1)} custom-call(f32[1088,128]{1,0:T(8,128)S(1)} %bitcast.10, bf16[9,128,768]{2,1,0:T(8,128)(2,1)S(1)} %copy-done), custom_call_target="tpu_custom_call" | custom-call | tf_op jit(solution)/shard_map/columns/pallas_call | solution.py:332
  33.4 0.0 copy-start.1
  33.4 0.0 copy-start.2
  33.4 0.0 copy-start.3
  33.4 0.0 copy-start.4
  33.4 40.6 %all_to_all.16 = f32[256,8,128]{2,1,0:T(8,128)S(1)} all-to-all(f32[256,8,128]{2,1,0:T(8,128)S(1)} %bitcast.6), channel_id=1, replica_groups=mesh['gy'=16,'gz'=16] {'gy','gz'}, dimensions={0} | all-to-all | bytes 2097152 | tf_op jit(solution)/shard_map/all_to_all | solution.py:341
  74.0 0.0 copy-done.1
  74.0 0.0 copy-done.2
  74.0 0.0 copy-done.3
  74.0 0.0 copy-done.4
  74.0 1.8 %modes.1 = f32[1536,128]{1,0:T(8,128)S(1)} custom-call(f32[2048,128]{1,0:T(8,128)S(1)} %bitcast.7, bf16[768,256]{1,0:T(8,128)(2,1)S(1)} %copy-done.1, f32[128,256]{1,0:T(8,128)S(1)} %copy-done.4, f32[128,256]{1,0:T(8,128)S(1)} %copy-done.3, bf16[128,768]{1,0:T(8,128)(2,1)S(1)} %copy-done.2), custom_call_target="tpu_custom_call" | custom-call | tf_op jit(solution)/shard_map/modes/pallas_call | solution.py:343
  75.8 18.8 %all_to_all.17 = f32[16,96,128]{2,1,0:T(8,128)S(1)} all-to-all(f32[16,96,128]{2,1,0:T(8,128)S(1)} %bitcast.9), channel_id=1, replica_groups=mesh['gy'=16,'gz'=16] {'gy'}, dimensions={0} | all-to-all | bytes 1572864 | tf_op jit(solution)/shard_map/all_to_all | solution.py:351
  94.6 1.4 %spectra.1 = f32[4,2,256,128]{3,2,1,0:T(8,128)} custom-call(f32[1536,128]{1,0:T(8,128)S(1)} %bitcast.8), custom_call_target="tpu_custom_call" | custom-call | tf_op jit(solution)/shard_map/spectra/pallas_call | solution.py:352
Async XLA Ops:
  0.0 32.0 %copy-start = (bf16[9,128,768]{2,1,0:T(8,128)(2,1)S(1)}, bf16[9,128,768]{2,1,0:T(8,128)(2,1)}, u32[]{:S(2)}) copy-start(bf16[9,128,768]{2,1,0:T(8,128)(2,1)} %constant.10.clone.w_ref) | copy-start | bytes 5308420
  0.9 5.5 %collective-permute-start = (s32[6,4,128]{2,1,0:T(4,128)S(1)}, s32[6,4,128]{2,1,0:T(4,128)S(1)}, u32[]{:S(2)}, u32[]{:S(2)}) collective-permute-start(s32[6,4,128]{2,1,0:T(4,128)S(1)} %slice.3), channel_id=1, source_target_pairs={{16,0},{32,16},{48,32},{64,48},{80,64},{96,80},{112,96},{128,112},... | collective-permute-start | bytes 36872 | tf_op jit(solution)/shard_map/ppermute | solution.py:306
  33.4 40.6 %copy-start.1 = (bf16[768,256]{1,0:T(8,128)(2,1)S(1)}, bf16[768,256]{1,0:T(8,128)(2,1)}, u32[]{:S(2)}) copy-start(bf16[768,256]{1,0:T(8,128)(2,1)} %constant.11.clone.y_ref) | copy-start | bytes 1179652
  33.4 40.6 %copy-start.2 = (bf16[128,768]{1,0:T(8,128)(2,1)S(1)}, bf16[128,768]{1,0:T(8,128)(2,1)}, u32[]{:S(2)}) copy-start(bf16[128,768]{1,0:T(8,128)(2,1)} %constant.14.clone.last_ref) | copy-start | bytes 589828
  33.4 40.6 %copy-start.3 = (f32[128,256]{1,0:T(8,128)S(1)}, f32[128,256]{1,0:T(8,128)}, u32[]{:S(2)}) copy-start(f32[128,256]{1,0:T(8,128)} %constant.13.clone.ti_ref) | copy-start | bytes 393220
  33.4 40.6 %copy-start.4 = (f32[128,256]{1,0:T(8,128)S(1)}, f32[128,256]{1,0:T(8,128)}, u32[]{:S(2)}) copy-start(f32[128,256]{1,0:T(8,128)} %constant.12.clone.tr_ref) | copy-start | bytes 393220

commit v8 on v7

--- a/solution.py
+++ b/solution.py
@@ -120,44 +120,42 @@
     for k in range(6):
         table_ref[k : k + 1, :] = jnp.full((1, 128), values[k], jnp.float32)
     table_ref[6:8, :] = jnp.zeros((2, 128), jnp.float32)
-    done = 0
+    done = 1
     for b in range(BLOCKS):
         copies[1 + b].wait()
         rows = pl.ds(TALL * b, TALL)
         for a, value in enumerate(along_x([fill(values, held[x, rows, :]) for x in range(6)])):
             ext[a, rows, :] = value
-        ready = (TALL * (b + 1) - 3) // 16
+        ready = TALL * (b + 1) // 16
         for a in range(4):
             for d in range(done, ready):
                 at = CHUNK * d + 16 * a
-                out_ref[at : at + 16, :] = along_y(ext, a, 16 * d, 16)
+                out_ref[at : at + 16, :] = along_y(ext, a, 16 * d - 4, 16)
         done = ready
     for p in range(2):
         a = 2 + p
-        for d in range(15):
+        for d in range(1, 16):
             at = CHUNK * d + 16 * a
             edge = CHUNK * d + 64 + 2 * p
-            below = along_y(ext, a, -1, 1) if d == 0 else out_ref[at - CHUNK + 15 : at - CHUNK + 16, :]
-            above = along_y(ext, a, 240, 1) if d == 14 else out_ref[at + CHUNK : at + CHUNK + 1, :]
+            below = along_y(ext, a, 11, 1) if d == 1 else out_ref[at - CHUNK + 15 : at - CHUNK + 16, :]
+            above = along_y(ext, a, 252, 1) if d == 15 else out_ref[at + CHUNK : at + CHUNK + 1, :]
             out_ref[edge : edge + 1, :] = below
             out_ref[edge + 1 : edge + 2, :] = above
-    out_ref[15 * CHUNK :, :] = jnp.zeros((CHUNK, 128), jnp.float32)
-    end_ref[...] = ext[:, 232:256, :]
-
-
-def rows_kernel(in_ref, end_ref, table_ref, next_ref, out_ref, ext):
-    last = 15 * CHUNK
-    out_ref[:last, :] = in_ref[:last, :]
-    ext[:, 0:24, :] = end_ref[...]
+    out_ref[:CHUNK, :] = jnp.zeros((CHUNK, 128), jnp.float32)
+    end_ref[...] = ext[:, 0:24, :]
+
+
+def rows_kernel(in_ref, end_ref, table_ref, before_ref, out_ref, ext):
+    out_ref[CHUNK:, :] = in_ref[CHUNK:, :]
+    ext[:, 8:32, :] = end_ref[...]
     values = [table_ref[k : k + 1, :] for k in range(6)]
-    for a, value in enumerate(along_x([fill(values, next_ref[x]) for x in range(6)])):
-        ext[a, 24:28, :] = value
-        out_ref[last + 16 * a : last + 16 * a + 16, :] = along_y(ext, a, 8, 16)
+    for a, value in enumerate(along_x([fill(values, before_ref[x]) for x in range(6)])):
+        ext[a, 4:8, :] = value
+        out_ref[16 * a : 16 * a + 16, :] = along_y(ext, a, 4, 16)
     for p in range(2):
-        a = 2 + p
-        edge = last + 64 + 2 * p
-        out_ref[edge : edge + 1, :] = along_y(ext, a, 7, 1)
-        out_ref[edge + 1 : edge + 2, :] = along_y(ext, a, 24, 1)
+        edge = 64 + 2 * p
+        out_ref[edge : edge + 1, :] = along_y(ext, 2 + p, 3, 1)
+        out_ref[edge + 1 : edge + 2, :] = along_y(ext, 2 + p, 20, 1)
 
 
 def real_transform(x):
@@ -303,7 +301,7 @@
 
 def shards(labels, porosity):
     count = lax.axis_size("gy")
-    following = lax.ppermute(labels[:, :4, :], "gy", [((i + 1) % count, i) for i in range(count)])
+    preceding = lax.ppermute(labels[:, -4:, :], "gy", [(i, (i + 1) % count) for i in range(count)])
     planes, ends, table = pl.pallas_call(
         planes_kernel,
         out_shape=(shape(16 * CHUNK, 128), shape(4, 24, 128), shape(8, 128)),
@@ -327,7 +325,7 @@
         scratch_shapes=[pltpu.VMEM((4, 32, 128), jnp.float32)],
         compiler_params=PARAMS,
         name="rows",
-    )(planes, ends, table, following)
+    )(planes, ends, table, preceding)
     rows = lax.all_to_all(rows.reshape(4 * CHUNK, 4, 128), "gz", 0, 0, tiled=True).reshape(16 * CHUNK, 128)
     columns = pl.pallas_call(
         columns_kernel,

time: 96.2 us -> 96.9 us (level)
    all_to_all x1, blocking collectives: 40.6 us -> 44 us  [shards(): lax.all_to_all(columns.reshape(256, 8, 128), ('gy', 'gz'), 0, 0, tiled=True)]
    all_to_all x1, blocking collectives: 25.6 us -> 22.8 us  [shards(): lax.all_to_all(rows.reshape(4 * CHUNK, 4, 128), 'gz', 0, 0, tiled=True)]
  transfers between devices with their start and end apart: 1 -> 1, of which waited for: 1 -> 0; matrix products, arithmetic and copies ran while one was open for 0% -> 0% of each run, Pallas kernels for 1% -> 1%
where the time goes in v8:
time: 96.9 us; the launch traced here: 96.7 us
  blocking collectives  85.6 us (88%)
  Pallas kernels  6.01 us (6%)
  starting transfers between devices  4.13 us (4%)
    all_to_all x1, blocking collectives, shards(): lax.all_to_all(columns.reshape(256, 8, 128), ('gy', 'gz'), 0, 0, tiled=True)  44 us
    all_to_all x1, blocking collectives, shards(): lax.all_to_all(rows.reshape(4 * CHUNK, 4, 128), 'gz', 0, 0, tiled=True)  22.8 us
    all_to_all x1, blocking collectives, shards(): modes = lax.all_to_all(modes.reshape(16, 96, 128), 'gy', 0, 0, tiled=True)  18.8 us
    ppermute x1, starting transfers between devices, shards(): lax.ppermute(labels[:, -4:, :], 'gy', [(i, (i + 1) % count) for i in rang...  4.13 us
  transfers between devices with their start and end apart: 1, of which 0 were waited for; matrix products, arithmetic and copies ran while one was open for 0% of the time, Pallas kernels for 1%

profile of v8, /device:TPU:1, one launch (start us, length us, event | category | flops | bytes accessed | tf_op | source)
XLA Modules:
  0.0 96.7 jit_solution(3522798198812454625)
XLA Ops:
  0.0 0.0 copy-start
  0.0 0.9 slice.3
  0.9 4.1 %collective-permute-start = (s32[6,4,128]{2,1,0:T(4,128)S(1)}, s32[6,4,128]{2,1,0:T(4,128)S(1)}, u32[]{:S(2)}, u32[]{:S(2)}) collective-permute-start(s32[6,4,128]{2,1,0:T(4,128)S(1)} %slice.3), channel_id=1, source_target_pairs={{0,16},{16,32},{32,48},{48,64},{64,80},{80,96},{96,112},{112,128},... | collective-permute-start | bytes 36872 | tf_op jit(solution)/shard_map/ppermute | solution.py:304
  5.0 1.4 %planes.1 = (f32[1088,128]{1,0:T(8,128)S(1)}, f32[4,24,128]{2,1,0:T(8,128)S(1)}, f32[8,128]{1,0:T(8,128)S(1)}) custom-call(f32[6]{0:T(128)} %por_ref.1, s32[6,256,128]{2,1,0:T(8,128)} %lab_ref.1), custom_call_target="tpu_custom_call" | custom-call | flops 10000000 | bytes 4000000 | tf_op jit(solution)/shard_map/planes/pallas_call | solution.py:305
  6.4 0.0 collective-permute-done.before_ref
  6.5 0.1 rows.1
  6.5 22.8 %all_to_all.15 = f32[272,4,128]{2,1,0:T(4,128)S(1)} all-to-all(f32[272,4,128]{2,1,0:T(4,128)S(1)} %bitcast.11), channel_id=1, replica_groups=mesh['gy'=16,'gz'=16] {'gz'}, dimensions={0} | all-to-all | bytes 1114112 | tf_op jit(solution)/shard_map/all_to_all | solution.py:329
  29.3 0.0 copy-done
  29.3 1.4 %columns.1 = f32[16,128,128]{2,1,0:T(8,128)S(1)} custom-call(f32[1088,128]{1,0:T(8,128)S(1)} %bitcast.10, bf16[9,128,768]{2,1,0:T(8,128)(2,1)S(1)} %copy-done), custom_call_target="tpu_custom_call" | custom-call | tf_op jit(solution)/shard_map/columns/pallas_call | solution.py:330
  30.7 0.0 copy-start.1
  30.7 0.0 copy-start.2
  30.7 0.0 copy-start.3
  30.7 0.0 copy-start.4
  30.7 44.0 %all_to_all.16 = f32[256,8,128]{2,1,0:T(8,128)S(1)} all-to-all(f32[256,8,128]{2,1,0:T(8,128)S(1)} %bitcast.6), channel_id=1, replica_groups=mesh['gy'=16,'gz'=16] {'gy','gz'}, dimensions={0} | all-to-all | bytes 2097152 | tf_op jit(solution)/shard_map/all_to_all | solution.py:339
  74.7 0.0 copy-done.1
  74.7 0.0 copy-done.2
  74.7 0.0 copy-done.3
  74.7 0.0 copy-done.4
  74.7 1.8 %modes.1 = f32[1536,128]{1,0:T(8,128)S(1)} custom-call(f32[2048,128]{1,0:T(8,128)S(1)} %bitcast.7, bf16[768,256]{1,0:T(8,128)(2,1)S(1)} %copy-done.1, f32[128,256]{1,0:T(8,128)S(1)} %copy-done.4, f32[128,256]{1,0:T(8,128)S(1)} %copy-done.3, bf16[128,768]{1,0:T(8,128)(2,1)S(1)} %copy-done.2), custom_call_target="tpu_custom_call" | custom-call | tf_op jit(solution)/shard_map/modes/pallas_call | solution.py:341
  76.5 18.8 %all_to_all.17 = f32[16,96,128]{2,1,0:T(8,128)S(1)} all-to-all(f32[16,96,128]{2,1,0:T(8,128)S(1)} %bitcast.9), channel_id=1, replica_groups=mesh['gy'=16,'gz'=16] {'gy'}, dimensions={0} | all-to-all | bytes 1572864 | tf_op jit(solution)/shard_map/all_to_all | solution.py:349
  95.3 1.4 %spectra.1 = f32[4,2,256,128]{3,2,1,0:T(8,128)} custom-call(f32[1536,128]{1,0:T(8,128)S(1)} %bitcast.8), custom_call_target="tpu_custom_call" | custom-call | tf_op jit(solution)/shard_map/spectra/pallas_call | solution.py:350
Async XLA Ops:
  0.0 29.3 %copy-start = (bf16[9,128,768]{2,1,0:T(8,128)(2,1)S(1)}, bf16[9,128,768]{2,1,0:T(8,128)(2,1)}, u32[]{:S(2)}) copy-start(bf16[9,128,768]{2,1,0:T(8,128)(2,1)} %constant.10.clone.w_ref) | copy-start | bytes 5308420
  0.9 5.6 %collective-permute-start = (s32[6,4,128]{2,1,0:T(4,128)S(1)}, s32[6,4,128]{2,1,0:T(4,128)S(1)}, u32[]{:S(2)}, u32[]{:S(2)}) collective-permute-start(s32[6,4,128]{2,1,0:T(4,128)S(1)} %slice.3), channel_id=1, source_target_pairs={{0,16},{16,32},{32,48},{48,64},{64,80},{80,96},{96,112},{112,128},... | collective-permute-start | bytes 36872 | tf_op jit(solution)/shard_map/ppermute | solution.py:304
  30.7 44.1 %copy-start.1 = (bf16[768,256]{1,0:T(8,128)(2,1)S(1)}, bf16[768,256]{1,0:T(8,128)(2,1)}, u32[]{:S(2)}) copy-start(bf16[768,256]{1,0:T(8,128)(2,1)} %constant.11.clone.y_ref) | copy-start | bytes 1179652
  30.7 44.0 %copy-start.2 = (bf16[128,768]{1,0:T(8,128)(2,1)S(1)}, bf16[128,768]{1,0:T(8,128)(2,1)}, u32[]{:S(2)}) copy-start(bf16[128,768]{1,0:T(8,128)(2,1)} %constant.14.clone.last_ref) | copy-start | bytes 589828
  30.7 44.0 %copy-start.3 = (f32[128,256]{1,0:T(8,128)S(1)}, f32[128,256]{1,0:T(8,128)}, u32[]{:S(2)}) copy-start(f32[128,256]{1,0:T(8,128)} %constant.13.clone.ti_ref) | copy-start | bytes 393220
  30.7 44.0 %copy-start.4 = (f32[128,256]{1,0:T(8,128)S(1)}, f32[128,256]{1,0:T(8,128)}, u32[]{:S(2)}) copy-start(f32[128,256]{1,0:T(8,128)} %constant.12.clone.tr_ref) | copy-start | bytes 393220

commit v9 on v7

--- a/solution.py
+++ b/solution.py
@@ -150,7 +150,7 @@
     out_ref[:last, :] = in_ref[:last, :]
     ext[:, 0:24, :] = end_ref[...]
     values = [table_ref[k : k + 1, :] for k in range(6)]
-    for a, value in enumerate(along_x([fill(values, next_ref[x]) for x in range(6)])):
+    for a, value in enumerate(along_x([fill(values, next_ref[x, 0:4, :]) for x in range(6)])):
         ext[a, 24:28, :] = value
         out_ref[last + 16 * a : last + 16 * a + 16, :] = along_y(ext, a, 8, 16)
     for p in range(2):
@@ -303,7 +303,7 @@
 
 def shards(labels, porosity):
     count = lax.axis_size("gy")
-    following = lax.ppermute(labels[:, :4, :], "gy", [((i + 1) % count, i) for i in range(count)])
+    following = lax.ppermute(labels[:, :8, :], "gy", [((i + 1) % count, i) for i in range(count)])
     planes, ends, table = pl.pallas_call(
         planes_kernel,
         out_shape=(shape(16 * CHUNK, 128), shape(4, 24, 128), shape(8, 128)),

time: 96.2 us -> 96.2 us (level)
  no operation moved by 1% of the time
where the time goes in v9:
time: 96.2 us; the launch traced here: 96 us
  blocking collectives  84.8 us (88%)
  Pallas kernels  6 us (6%)
  starting transfers between devices  3.24 us (3%)
  waiting for transfers between devices  0.97 us (1%)
    all_to_all x1, blocking collectives, shards(): lax.all_to_all(columns.reshape(256, 8, 128), ('gy', 'gz'), 0, 0, tiled=True)  40.4 us
    all_to_all x1, blocking collectives, shards(): lax.all_to_all(rows.reshape(4 * CHUNK, 4, 128), 'gz', 0, 0, tiled=True)  25.6 us
    all_to_all x1, blocking collectives, shards(): modes = lax.all_to_all(modes.reshape(16, 96, 128), 'gy', 0, 0, tiled=True)  18.8 us
    ppermute x1, starting transfers between devices, shards(): lax.ppermute(labels[:, :8, :], 'gy', [((i + 1) % count, i) for i in range...  3.24 us
  transfers between devices with their start and end apart: 1, of which 1 were waited for; matrix products, arithmetic and copies ran while one was open for 0% of the time, Pallas kernels for 1%

profile of v9, /device:TPU:1, one launch (start us, length us, event | category | flops | bytes accessed | tf_op | source)
XLA Modules:
  0.0 96.0 jit_solution(6833684125130076108)
XLA Ops:
  0.0 0.0 copy-start
  0.0 0.9 slice.3
  0.9 3.2 %collective-permute-start = (s32[6,8,128]{2,1,0:T(8,128)S(1)}, s32[6,8,128]{2,1,0:T(8,128)S(1)}, u32[]{:S(2)}, u32[]{:S(2)}) collective-permute-start(s32[6,8,128]{2,1,0:T(8,128)S(1)} %slice.3), channel_id=1, source_target_pairs={{16,0},{32,16},{48,32},{64,48},{80,64},{96,80},{112,96},{128,112},... | collective-permute-start | bytes 73736 | tf_op jit(solution)/shard_map/ppermute | solution.py:306
  4.1 1.4 %planes.1 = (f32[1088,128]{1,0:T(8,128)S(1)}, f32[4,24,128]{2,1,0:T(8,128)S(1)}, f32[8,128]{1,0:T(8,128)S(1)}) custom-call(f32[6]{0:T(128)} %por_ref.1, s32[6,256,128]{2,1,0:T(8,128)} %lab_ref.1), custom_call_target="tpu_custom_call" | custom-call | flops 10000000 | bytes 4000000 | tf_op jit(solution)/shard_map/planes/pallas_call | solution.py:307
  5.5 1.0 %collective-permute-done.next_ref = s32[6,8,128]{2,1,0:T(8,128)S(1)} collective-permute-done((s32[6,8,128]{2,1,0:T(8,128)S(1)}, s32[6,8,128]{2,1,0:T(8,128)S(1)}, u32[]{:S(2)}, u32[]{:S(2)}) %collective-permute-start) | collective-permute-done | bytes 24608 | tf_op jit(solution)/shard_map/ppermute | solution.py:306
  6.5 0.1 rows.1
  6.6 25.6 %all_to_all.15 = f32[272,4,128]{2,1,0:T(4,128)S(1)} all-to-all(f32[272,4,128]{2,1,0:T(4,128)S(1)} %bitcast.11), channel_id=1, replica_groups=mesh['gy'=16,'gz'=16] {'gz'}, dimensions={0} | all-to-all | bytes 1114112 | tf_op jit(solution)/shard_map/all_to_all | solution.py:331
  32.2 0.0 copy-done
  32.2 1.4 %columns.1 = f32[16,128,128]{2,1,0:T(8,128)S(1)} custom-call(f32[1088,128]{1,0:T(8,128)S(1)} %bitcast.10, bf16[9,128,768]{2,1,0:T(8,128)(2,1)S(1)} %copy-done), custom_call_target="tpu_custom_call" | custom-call | tf_op jit(solution)/shard_map/columns/pallas_call | solution.py:332
  33.6 0.0 copy-start.1
  33.6 0.0 copy-start.2
  33.6 0.0 copy-start.3
  33.6 0.0 copy-start.4
  33.6 40.4 %all_to_all.16 = f32[256,8,128]{2,1,0:T(8,128)S(1)} all-to-all(f32[256,8,128]{2,1,0:T(8,128)S(1)} %bitcast.6), channel_id=1, replica_groups=mesh['gy'=16,'gz'=16] {'gy','gz'}, dimensions={0} | all-to-all | bytes 2097152 | tf_op jit(solution)/shard_map/all_to_all | solution.py:341
  74.1 0.0 copy-done.1
  74.1 0.0 copy-done.2
  74.1 0.0 copy-done.3
  74.1 0.0 copy-done.4
  74.1 1.8 %modes.1 = f32[1536,128]{1,0:T(8,128)S(1)} custom-call(f32[2048,128]{1,0:T(8,128)S(1)} %bitcast.7, bf16[768,256]{1,0:T(8,128)(2,1)S(1)} %copy-done.1, f32[128,256]{1,0:T(8,128)S(1)} %copy-done.4, f32[128,256]{1,0:T(8,128)S(1)} %copy-done.3, bf16[128,768]{1,0:T(8,128)(2,1)S(1)} %copy-done.2), custom_call_target="tpu_custom_call" | custom-call | tf_op jit(solution)/shard_map/modes/pallas_call | solution.py:343
  75.9 18.8 %all_to_all.17 = f32[16,96,128]{2,1,0:T(8,128)S(1)} all-to-all(f32[16,96,128]{2,1,0:T(8,128)S(1)} %bitcast.9), channel_id=1, replica_groups=mesh['gy'=16,'gz'=16] {'gy'}, dimensions={0} | all-to-all | bytes 1572864 | tf_op jit(solution)/shard_map/all_to_all | solution.py:351
  94.7 1.4 %spectra.1 = f32[4,2,256,128]{3,2,1,0:T(8,128)} custom-call(f32[1536,128]{1,0:T(8,128)S(1)} %bitcast.8), custom_call_target="tpu_custom_call" | custom-call | tf_op jit(solution)/shard_map/spectra/pallas_call | solution.py:352
Async XLA Ops:
  0.0 32.2 %copy-start = (bf16[9,128,768]{2,1,0:T(8,128)(2,1)S(1)}, bf16[9,128,768]{2,1,0:T(8,128)(2,1)}, u32[]{:S(2)}) copy-start(bf16[9,128,768]{2,1,0:T(8,128)(2,1)} %constant.10.clone.w_ref) | copy-start | bytes 5308420
  0.9 5.6 %collective-permute-start = (s32[6,8,128]{2,1,0:T(8,128)S(1)}, s32[6,8,128]{2,1,0:T(8,128)S(1)}, u32[]{:S(2)}, u32[]{:S(2)}) collective-permute-start(s32[6,8,128]{2,1,0:T(8,128)S(1)} %slice.3), channel_id=1, source_target_pairs={{16,0},{32,16},{48,32},{64,48},{80,64},{96,80},{112,96},{128,112},... | collective-permute-start | bytes 73736 | tf_op jit(solution)/shard_map/ppermute | solution.py:306
  33.6 40.5 %copy-start.1 = (bf16[768,256]{1,0:T(8,128)(2,1)S(1)}, bf16[768,256]{1,0:T(8,128)(2,1)}, u32[]{:S(2)}) copy-start(bf16[768,256]{1,0:T(8,128)(2,1)} %constant.11.clone.y_ref) | copy-start | bytes 1179652
  33.6 40.5 %copy-start.2 = (bf16[128,768]{1,0:T(8,128)(2,1)S(1)}, bf16[128,768]{1,0:T(8,128)(2,1)}, u32[]{:S(2)}) copy-start(bf16[128,768]{1,0:T(8,128)(2,1)} %constant.14.clone.last_ref) | copy-start | bytes 589828
  33.6 40.5 %copy-start.3 = (f32[128,256]{1,0:T(8,128)S(1)}, f32[128,256]{1,0:T(8,128)}, u32[]{:S(2)}) copy-start(f32[128,256]{1,0:T(8,128)} %constant.13.clone.ti_ref) | copy-start | bytes 393220
  33.6 40.5 %copy-start.4 = (f32[128,256]{1,0:T(8,128)S(1)}, f32[128,256]{1,0:T(8,128)}, u32[]{:S(2)}) copy-start(f32[128,256]{1,0:T(8,128)} %constant.12.clone.tr_ref) | copy-start | bytes 393220

commit v10 on v7

--- a/solution.py
+++ b/solution.py
@@ -209,7 +209,8 @@
         grad_y = along_z(ext[:, 9:25, :] - ext[:, 7:23, :])
         pore = along_z(center)
         grad_z = after(pore) - before(pore)
-        surface = jnp.sqrt(grad_x * grad_x + grad_y * grad_y + grad_z * grad_z + 0.01)
+        square = grad_x * grad_x + grad_y * grad_y + grad_z * grad_z + 0.01
+        surface = square * lax.rsqrt(square)
         x_ref[:, 16 * p : 16 * p + 16, :] = surface
         x_ref[:, 32 + 16 * p : 48 + 16 * p, :] = pore
     parts = real_transform([x_ref[d] for d in range(16)])

time: 96.2 us -> 96.1 us (level)
  no operation moved by 1% of the time
where the time goes in v10:
time: 96.1 us; the launch traced here: 95.9 us
  blocking collectives  84.9 us (88%)
  Pallas kernels  5.97 us (6%)
  starting transfers between devices  3.24 us (3%)
    all_to_all x1, blocking collectives, shards(): lax.all_to_all(columns.reshape(256, 8, 128), ('gy', 'gz'), 0, 0, tiled=True)  40.6 us
    all_to_all x1, blocking collectives, shards(): lax.all_to_all(rows.reshape(4 * CHUNK, 4, 128), 'gz', 0, 0, tiled=True)  25.6 us
    all_to_all x1, blocking collectives, shards(): modes = lax.all_to_all(modes.reshape(16, 96, 128), 'gy', 0, 0, tiled=True)  18.8 us
    ppermute x1, starting transfers between devices, shards(): lax.ppermute(labels[:, :4, :], 'gy', [((i + 1) % count, i) for i in range...  3.24 us
  transfers between devices with their start and end apart: 1, of which 1 were waited for; matrix products, arithmetic and copies ran while one was open for 0% of the time, Pallas kernels for 1%

profile of v10, /device:TPU:1, one launch (start us, length us, event | category | flops | bytes accessed | tf_op | source)
XLA Modules:
  0.0 95.9 jit_solution(14089310650680993146)
XLA Ops:
  0.0 0.0 copy-start
  0.0 0.9 slice.3
  0.9 3.2 %collective-permute-start = (s32[6,4,128]{2,1,0:T(4,128)S(1)}, s32[6,4,128]{2,1,0:T(4,128)S(1)}, u32[]{:S(2)}, u32[]{:S(2)}) collective-permute-start(s32[6,4,128]{2,1,0:T(4,128)S(1)} %slice.3), channel_id=1, source_target_pairs={{16,0},{32,16},{48,32},{64,48},{80,64},{96,80},{112,96},{128,112},... | collective-permute-start | bytes 36872 | tf_op jit(solution)/shard_map/ppermute | solution.py:307
  4.1 1.4 %planes.1 = (f32[1088,128]{1,0:T(8,128)S(1)}, f32[4,24,128]{2,1,0:T(8,128)S(1)}, f32[8,128]{1,0:T(8,128)S(1)}) custom-call(f32[6]{0:T(128)} %por_ref.1, s32[6,256,128]{2,1,0:T(8,128)} %lab_ref.1), custom_call_target="tpu_custom_call" | custom-call | flops 10000000 | bytes 4000000 | tf_op jit(solution)/shard_map/planes/pallas_call | solution.py:308
  5.5 0.8 collective-permute-done.next_ref
  6.4 0.1 rows.1
  6.5 25.6 %all_to_all.15 = f32[272,4,128]{2,1,0:T(4,128)S(1)} all-to-all(f32[272,4,128]{2,1,0:T(4,128)S(1)} %bitcast.11), channel_id=1, replica_groups=mesh['gy'=16,'gz'=16] {'gz'}, dimensions={0} | all-to-all | bytes 1114112 | tf_op jit(solution)/shard_map/all_to_all | solution.py:332
  32.0 0.0 copy-done
  32.0 1.3 %columns.1 = f32[16,128,128]{2,1,0:T(8,128)S(1)} custom-call(f32[1088,128]{1,0:T(8,128)S(1)} %bitcast.10, bf16[9,128,768]{2,1,0:T(8,128)(2,1)S(1)} %copy-done), custom_call_target="tpu_custom_call" | custom-call | tf_op jit(solution)/shard_map/columns/pallas_call | solution.py:333
  33.3 0.0 copy-start.1
  33.3 0.0 copy-start.2
  33.4 0.0 copy-start.3
  33.4 0.0 copy-start.4
  33.4 40.6 %all_to_all.16 = f32[256,8,128]{2,1,0:T(8,128)S(1)} all-to-all(f32[256,8,128]{2,1,0:T(8,128)S(1)} %bitcast.6), channel_id=1, replica_groups=mesh['gy'=16,'gz'=16] {'gy','gz'}, dimensions={0} | all-to-all | bytes 2097152 | tf_op jit(solution)/shard_map/all_to_all | solution.py:342
  73.9 0.0 copy-done.1
  73.9 0.0 copy-done.2
  73.9 0.0 copy-done.3
  73.9 0.0 copy-done.4
  74.0 1.8 %modes.1 = f32[1536,128]{1,0:T(8,128)S(1)} custom-call(f32[2048,128]{1,0:T(8,128)S(1)} %bitcast.7, bf16[768,256]{1,0:T(8,128)(2,1)S(1)} %copy-done.1, f32[128,256]{1,0:T(8,128)S(1)} %copy-done.4, f32[128,256]{1,0:T(8,128)S(1)} %copy-done.3, bf16[128,768]{1,0:T(8,128)(2,1)S(1)} %copy-done.2), custom_call_target="tpu_custom_call" | custom-call | tf_op jit(solution)/shard_map/modes/pallas_call | solution.py:344
  75.7 18.8 %all_to_all.17 = f32[16,96,128]{2,1,0:T(8,128)S(1)} all-to-all(f32[16,96,128]{2,1,0:T(8,128)S(1)} %bitcast.9), channel_id=1, replica_groups=mesh['gy'=16,'gz'=16] {'gy'}, dimensions={0} | all-to-all | bytes 1572864 | tf_op jit(solution)/shard_map/all_to_all | solution.py:352
  94.5 1.4 %spectra.1 = f32[4,2,256,128]{3,2,1,0:T(8,128)} custom-call(f32[1536,128]{1,0:T(8,128)S(1)} %bitcast.8), custom_call_target="tpu_custom_call" | custom-call | tf_op jit(solution)/shard_map/spectra/pallas_call | solution.py:353
Async XLA Ops:
  0.0 32.0 %copy-start = (bf16[9,128,768]{2,1,0:T(8,128)(2,1)S(1)}, bf16[9,128,768]{2,1,0:T(8,128)(2,1)}, u32[]{:S(2)}) copy-start(bf16[9,128,768]{2,1,0:T(8,128)(2,1)} %constant.10.clone.w_ref) | copy-start | bytes 5308420
  0.9 5.5 %collective-permute-start = (s32[6,4,128]{2,1,0:T(4,128)S(1)}, s32[6,4,128]{2,1,0:T(4,128)S(1)}, u32[]{:S(2)}, u32[]{:S(2)}) collective-permute-start(s32[6,4,128]{2,1,0:T(4,128)S(1)} %slice.3), channel_id=1, source_target_pairs={{16,0},{32,16},{48,32},{64,48},{80,64},{96,80},{112,96},{128,112},... | collective-permute-start | bytes 36872 | tf_op jit(solution)/shard_map/ppermute | solution.py:307
  33.3 40.6 %copy-start.1 = (bf16[768,256]{1,0:T(8,128)(2,1)S(1)}, bf16[768,256]{1,0:T(8,128)(2,1)}, u32[]{:S(2)}) copy-start(bf16[768,256]{1,0:T(8,128)(2,1)} %constant.11.clone.y_ref) | copy-start | bytes 1179652
  33.3 40.6 %copy-start.2 = (bf16[128,768]{1,0:T(8,128)(2,1)S(1)}, bf16[128,768]{1,0:T(8,128)(2,1)}, u32[]{:S(2)}) copy-start(bf16[128,768]{1,0:T(8,128)(2,1)} %constant.14.clone.last_ref) | copy-start | bytes 589828
  33.4 40.6 %copy-start.3 = (f32[128,256]{1,0:T(8,128)S(1)}, f32[128,256]{1,0:T(8,128)}, u32[]{:S(2)}) copy-start(f32[128,256]{1,0:T(8,128)} %constant.13.clone.ti_ref) | copy-start | bytes 393220
  33.4 40.6 %copy-start.4 = (f32[128,256]{1,0:T(8,128)S(1)}, f32[128,256]{1,0:T(8,128)}, u32[]{:S(2)}) copy-start(f32[128,256]{1,0:T(8,128)} %constant.12.clone.tr_ref) | copy-start | bytes 393220

commit v11 on v10

--- a/solution.py
+++ b/solution.py
@@ -104,7 +104,7 @@
 
 
 CHUNK = 68
-BLOCKS = 4
+BLOCKS = 8
 TALL = 256 // BLOCKS
 
 

time: 96.1 us -> 96.2 us (level)
  transfers between devices with their start and end apart: 1 -> 1, of which waited for: 1 -> 1; matrix products, arithmetic and copies ran while one was open for 0% -> 0% of each run, Pallas kernels for 1% -> 2%
where the time goes in v11:
time: 96.2 us; the launch traced here: 95.9 us
  blocking collectives  84.9 us (88%)
  Pallas kernels  6.01 us (6%)
  starting transfers between devices  3.24 us (3%)
    all_to_all x1, blocking collectives, shards(): lax.all_to_all(columns.reshape(256, 8, 128), ('gy', 'gz'), 0, 0, tiled=True)  40.7 us
    all_to_all x1, blocking collectives, shards(): lax.all_to_all(rows.reshape(4 * CHUNK, 4, 128), 'gz', 0, 0, tiled=True)  25.5 us
    all_to_all x1, blocking collectives, shards(): modes = lax.all_to_all(modes.reshape(16, 96, 128), 'gy', 0, 0, tiled=True)  18.8 us
    ppermute x1, starting transfers between devices, shards(): lax.ppermute(labels[:, :4, :], 'gy', [((i + 1) % count, i) for i in range...  3.24 us
  transfers between devices with their start and end apart: 1, of which 1 were waited for; matrix products, arithmetic and copies ran while one was open for 0% of the time, Pallas kernels for 2%

profile of v11, /device:TPU:1, one launch (start us, length us, event | category | flops | bytes accessed | tf_op | source)
XLA Modules:
  0.0 95.9 jit_solution(3446132580078689005)
XLA Ops:
  0.0 0.0 copy-start
  0.0 0.9 slice.3
  0.9 3.2 %collective-permute-start = (s32[6,4,128]{2,1,0:T(4,128)S(1)}, s32[6,4,128]{2,1,0:T(4,128)S(1)}, u32[]{:S(2)}, u32[]{:S(2)}) collective-permute-start(s32[6,4,128]{2,1,0:T(4,128)S(1)} %slice.3), channel_id=1, source_target_pairs={{16,0},{32,16},{48,32},{64,48},{80,64},{96,80},{112,96},{128,112},... | collective-permute-start | bytes 36872 | tf_op jit(solution)/shard_map/ppermute | solution.py:307
  4.1 1.5 %planes.1 = (f32[1088,128]{1,0:T(8,128)S(1)}, f32[4,24,128]{2,1,0:T(8,128)S(1)}, f32[8,128]{1,0:T(8,128)S(1)}) custom-call(f32[6]{0:T(128)} %por_ref.1, s32[6,256,128]{2,1,0:T(8,128)} %lab_ref.1), custom_call_target="tpu_custom_call" | custom-call | flops 10000000 | bytes 4000000 | tf_op jit(solution)/shard_map/planes/pallas_call | solution.py:308
  5.6 0.8 collective-permute-done.next_ref
  6.4 0.1 rows.1
  6.5 25.5 %all_to_all.15 = f32[272,4,128]{2,1,0:T(4,128)S(1)} all-to-all(f32[272,4,128]{2,1,0:T(4,128)S(1)} %bitcast.11), channel_id=1, replica_groups=mesh['gy'=16,'gz'=16] {'gz'}, dimensions={0} | all-to-all | bytes 1114112 | tf_op jit(solution)/shard_map/all_to_all | solution.py:332
  31.9 0.0 copy-done
  31.9 1.3 %columns.1 = f32[16,128,128]{2,1,0:T(8,128)S(1)} custom-call(f32[1088,128]{1,0:T(8,128)S(1)} %bitcast.10, bf16[9,128,768]{2,1,0:T(8,128)(2,1)S(1)} %copy-done), custom_call_target="tpu_custom_call" | custom-call | tf_op jit(solution)/shard_map/columns/pallas_call | solution.py:333
  33.3 0.0 copy-start.1
  33.3 0.0 copy-start.2
  33.3 0.0 copy-start.3
  33.3 0.0 copy-start.4
  33.3 40.7 %all_to_all.16 = f32[256,8,128]{2,1,0:T(8,128)S(1)} all-to-all(f32[256,8,128]{2,1,0:T(8,128)S(1)} %bitcast.6), channel_id=1, replica_groups=mesh['gy'=16,'gz'=16] {'gy','gz'}, dimensions={0} | all-to-all | bytes 2097152 | tf_op jit(solution)/shard_map/all_to_all | solution.py:342
  74.0 0.0 copy-done.1
  74.0 0.0 copy-done.2
  74.0 0.0 copy-done.3
  74.0 0.0 copy-done.4
  74.0 1.8 %modes.1 = f32[1536,128]{1,0:T(8,128)S(1)} custom-call(f32[2048,128]{1,0:T(8,128)S(1)} %bitcast.7, bf16[768,256]{1,0:T(8,128)(2,1)S(1)} %copy-done.1, f32[128,256]{1,0:T(8,128)S(1)} %copy-done.4, f32[128,256]{1,0:T(8,128)S(1)} %copy-done.3, bf16[128,768]{1,0:T(8,128)(2,1)S(1)} %copy-done.2), custom_call_target="tpu_custom_call" | custom-call | tf_op jit(solution)/shard_map/modes/pallas_call | solution.py:344
  75.8 18.8 %all_to_all.17 = f32[16,96,128]{2,1,0:T(8,128)S(1)} all-to-all(f32[16,96,128]{2,1,0:T(8,128)S(1)} %bitcast.9), channel_id=1, replica_groups=mesh['gy'=16,'gz'=16] {'gy'}, dimensions={0} | all-to-all | bytes 1572864 | tf_op jit(solution)/shard_map/all_to_all | solution.py:352
  94.6 1.4 %spectra.1 = f32[4,2,256,128]{3,2,1,0:T(8,128)} custom-call(f32[1536,128]{1,0:T(8,128)S(1)} %bitcast.8), custom_call_target="tpu_custom_call" | custom-call | tf_op jit(solution)/shard_map/spectra/pallas_call | solution.py:353
Async XLA Ops:
  0.0 31.9 %copy-start = (bf16[9,128,768]{2,1,0:T(8,128)(2,1)S(1)}, bf16[9,128,768]{2,1,0:T(8,128)(2,1)}, u32[]{:S(2)}) copy-start(bf16[9,128,768]{2,1,0:T(8,128)(2,1)} %constant.10.clone.w_ref) | copy-start | bytes 5308420
  0.9 5.5 %collective-permute-start = (s32[6,4,128]{2,1,0:T(4,128)S(1)}, s32[6,4,128]{2,1,0:T(4,128)S(1)}, u32[]{:S(2)}, u32[]{:S(2)}) collective-permute-start(s32[6,4,128]{2,1,0:T(4,128)S(1)} %slice.3), channel_id=1, source_target_pairs={{16,0},{32,16},{48,32},{64,48},{80,64},{96,80},{112,96},{128,112},... | collective-permute-start | bytes 36872 | tf_op jit(solution)/shard_map/ppermute | solution.py:307
  33.3 40.7 %copy-start.1 = (bf16[768,256]{1,0:T(8,128)(2,1)S(1)}, bf16[768,256]{1,0:T(8,128)(2,1)}, u32[]{:S(2)}) copy-start(bf16[768,256]{1,0:T(8,128)(2,1)} %constant.11.clone.y_ref) | copy-start | bytes 1179652
  33.3 40.7 %copy-start.2 = (bf16[128,768]{1,0:T(8,128)(2,1)S(1)}, bf16[128,768]{1,0:T(8,128)(2,1)}, u32[]{:S(2)}) copy-start(bf16[128,768]{1,0:T(8,128)(2,1)} %constant.14.clone.last_ref) | copy-start | bytes 589828
  33.3 40.7 %copy-start.3 = (f32[128,256]{1,0:T(8,128)S(1)}, f32[128,256]{1,0:T(8,128)}, u32[]{:S(2)}) copy-start(f32[128,256]{1,0:T(8,128)} %constant.13.clone.ti_ref) | copy-start | bytes 393220
  33.3 40.7 %copy-start.4 = (f32[128,256]{1,0:T(8,128)S(1)}, f32[128,256]{1,0:T(8,128)}, u32[]{:S(2)}) copy-start(f32[128,256]{1,0:T(8,128)} %constant.12.clone.tr_ref) | copy-start | bytes 393220
